TPU v7x, 32 devices: a whole 2x2x4 slice. The times are simulated.
32 devices in a mesh: dp: 4 (over y, core), fsdp: 8 (over z, x).
Axes of the slice: x: 2, y: 2, z: 4, core: 2. Of those that a mesh axis runs over, the one named last changes fastest.
Arguments:
- hidden_in: bfloat16 [16384, 768], P(('dp', 'fsdp')), may hold values from -6 to 6
- output_grad: bfloat16 [16384, 768], P(('dp', 'fsdp')), may hold values from -6 to 6
- encoder_states: bfloat16 [64, 512, 768], P(('dp', 'fsdp')), may hold values from -6 to 6
- language_ids: int32 [64], P(('dp', 'fsdp')), may hold values from 0 to 7
- source_index: int32 [64], P(('dp', 'fsdp')), may hold values from 0 to 1
- bucket_ids: int32 [256, 256], replicated, may hold values from 0 to 31, as said below
- language_table: bfloat16 [8, 768], P(None, ('dp', 'fsdp')), may hold values from -3 to 3
- bucket_table: bfloat16 [32, 12], replicated, may hold values from -4 to 4
- self_gain: bfloat16 [768], P(('dp', 'fsdp')), may hold values from 0.5 to 1.5
- self_query: bfloat16 [768, 768], P(('dp', 'fsdp')), may hold values from -0.02734375 to 0.02734375
- self_key: bfloat16 [768, 768], P(('dp', 'fsdp')), may hold values from -0.21875 to 0.21875
- self_value: bfloat16 [768, 768], P(('dp', 'fsdp')), may hold values from -0.21875 to 0.21875
- self_out: bfloat16 [768, 768], P(('dp', 'fsdp')), may hold values from -1.25 to 1.25
- cross_gain: bfloat16 [768], P(('dp', 'fsdp')), may hold values from 0.5 to 1.5
- cross_query: bfloat16 [768, 768], P(('dp', 'fsdp')), may hold values from -0.02734375 to 0.02734375
- cross_key: bfloat16 [768, 768], P(('dp', 'fsdp')), may hold values from -0.21875 to 0.21875
- cross_value: bfloat16 [768, 768], P(('dp', 'fsdp')), may hold values from -0.21875 to 0.21875
- cross_out: bfloat16 [768, 768], P(('dp', 'fsdp')), may hold values from -1.75 to 1.75
- feed_gain: bfloat16 [768], P(('dp', 'fsdp')), may hold values from 0.5 to 1.5
- inner_weight: bfloat16 [768, 3072], P(('dp', 'fsdp')), may hold values from -0.21875 to 0.21875
- outer_weight: bfloat16 [3072, 768], P(('dp', 'fsdp')), may hold values from -0.109375 to 0.109375
Outputs:
- hidden_out: bfloat16 [16384, 768], P(('dp', 'fsdp'))
- hidden_in_grad: float32 [16384, 768], P(('dp', 'fsdp'))
- encoder_grad: float32 [64, 512, 768], P(('dp', 'fsdp'))
- language_table_grad: float32 [8, 768], P(None, ('dp', 'fsdp'))
- bucket_table_grad: float32 [32, 12], replicated
- self_gain_grad: float32 [768], P(('dp', 'fsdp'))
- self_query_grad: float32 [768, 768], P(('dp', 'fsdp'))
- self_key_grad: float32 [768, 768], P(('dp', 'fsdp'))
- self_value_grad: float32 [768, 768], P(('dp', 'fsdp'))
- self_out_grad: float32 [768, 768], P(('dp', 'fsdp'))
- cross_gain_grad: float32 [768], P(('dp', 'fsdp'))
- cross_query_grad: float32 [768, 768], P(('dp', 'fsdp'))
- cross_key_grad: float32 [768, 768], P(('dp', 'fsdp'))
- cross_value_grad: float32 [768, 768], P(('dp', 'fsdp'))
- cross_out_grad: float32 [768, 768], P(('dp', 'fsdp'))
- feed_gain_grad: float32 [768], P(('dp', 'fsdp'))
- inner_weight_grad: float32 [768, 3072], P(('dp', 'fsdp'))
- outer_weight_grad: float32 [3072, 768], P(('dp', 'fsdp'))
Inputs may be any that keep to these rules, and one draw needn't show every extreme that they name: bucket_ids[i, j] is the bucket of the distance between the positions of query i and key j, the positions rising by 1 or 2 from token to token; exact buckets below 16, logarithmic ones up to a distance of 128 and above; 0 where j > i.
All inputs are finite; a program needn't handle non-finite values.
Results may differ from a plain program's by a relative error of at most 0.019.
Values may be sent and summed in bfloat16 or wider, within the bound.
A program may use at most 192 MiB of HBM per device.

v0:
```python
import functools

import jax
import jax.numpy as jnp
from jax import lax
from jax.experimental import pallas as pl
from jax.experimental.pallas import tpu as pltpu
from jax.sharding import PartitionSpec as P

H = 12
HEAD = 64
SEQ_BLOCK = 2


EPSILON = 1e-06
PRECISE = lax.Precision.HIGHEST
NEGATIVE = -1e30


def to_low(value):
    return value.astype(jnp.bfloat16)


def norm_scale(hidden, gain):
    return hidden * lax.rsqrt(jnp.mean(hidden * hidden, axis=-1, keepdims=True) + EPSILON) * gain


def matmul(left, right):
    return jnp.dot(left, right, preferred_element_type=jnp.float32)


def left_product(left, right):
    return lax.dot_general(
        left, right, (((0,), (0,)), ((), ())), preferred_element_type=jnp.float32
    )


def right_product(left, right):
    return lax.dot_general(
        left, right, (((1,), (1,)), ((), ())), preferred_element_type=jnp.float32
    )


def split_heads(array):
    return array.reshape(array.shape[:-1] + (H, HEAD))


def score_block(queries, key_rows, offset):
    scores = jnp.einsum(
        "sqhe,skhe->shqk",
        split_heads(queries),
        split_heads(key_rows),
        preferred_element_type=jnp.float32,
    )
    return scores + offset


def attend_forward(queries, key_rows, value_rows, offset):
    scores = score_block(queries, key_rows, offset)
    top_score = jnp.max(scores, axis=-1, keepdims=True)
    log_total = top_score + jnp.log(jnp.sum(jnp.exp(scores - top_score), axis=-1, keepdims=True))
    weights = to_low(jnp.exp(scores - log_total))
    context = jnp.einsum(
        "shqk,skhe->sqhe", weights, split_heads(value_rows), preferred_element_type=jnp.float32
    )
    return (to_low(context).reshape(queries.shape), log_total)


def attend_backward(queries, key_rows, value_rows, offset, log_total, context_grad, with_bias):
    scores = score_block(queries, key_rows, offset)
    probs = jnp.exp(scores - log_total)
    weights = to_low(probs)
    grad_heads = split_heads(context_grad)
    value_grad = jnp.einsum(
        "shqk,sqhe->skhe", weights, grad_heads, preferred_element_type=jnp.float32
    )
    prob_grad = jnp.einsum(
        "sqhe,skhe->shqk", grad_heads, split_heads(value_rows), preferred_element_type=jnp.float32
    )
    score_grad = to_low(probs * (prob_grad - jnp.sum(probs * prob_grad, axis=-1, keepdims=True)))
    query_grad = jnp.einsum(
        "shqk,skhe->sqhe", score_grad, split_heads(key_rows), preferred_element_type=jnp.float32
    )
    key_grad = jnp.einsum(
        "shqk,sqhe->skhe", score_grad, split_heads(queries), preferred_element_type=jnp.float32
    )
    grads = (
        query_grad.reshape(queries.shape),
        key_grad.reshape(key_rows.shape),
        value_grad.reshape(value_rows.shape),
    )
    if with_bias:
        return grads + (jnp.sum(score_grad.astype(jnp.float32), axis=0),)
    return grads


MESH = pl.DeviceIdType.MESH
ALL = slice(None)


class Place:
    def __init__(self, sizes):
        self.ny, self.nz = sizes
        self.dp = lax.axis_index("dp")
        self.fs = lax.axis_index("fsdp")
        self.c, self.y = lax.rem(self.dp, 2), lax.div(self.dp, 2)
        self.x, self.z = lax.rem(self.fs, 2), lax.div(self.fs, 2)

    def size(self, dim):
        return {"c": 2, "x": 2, "y": self.ny, "z": self.nz}[dim]

    def at(self, dim):
        return {"c": self.c, "x": self.x, "y": self.y, "z": self.z}[dim]

    def device(self, dim, index):
        if dim == "c":
            return (self.y * 2 + index, self.fs)
        if dim == "y":
            return (index * 2 + self.c, self.fs)
        if dim == "x":
            return (self.dp, self.z * 2 + index)
        return (self.dp, index * 2 + self.x)


def neighbour_barrier(place, far=False):
    barrier = pltpu.get_barrier_semaphore()
    links = []
    for dim in "cxyz":
        here, size = place.at(dim), place.size(dim)
        reach = 1
        while reach < size and (reach == 1 or far):
            if size == 2:
                links.append((dim, 1 - here, None))
            elif reach == 1:
                for step in (1, -1):
                    links.append((dim, here + step, (here + step >= 0) & (here + step < size)))
            else:
                links.append((dim, here + reach - 2 * reach * lax.rem(lax.div(here, reach), 2), None))
            reach *= 2

    def signal(dim, there):
        pl.semaphore_signal(barrier, inc=1, device_id=place.device(dim, there), device_id_type=MESH)

    for dim, there, condition in links:
        if condition is None:
            signal(dim, there)
        else:
            pl.when(condition)(lambda dim=dim, there=there: signal(dim, there))
    peers = sum(1 if condition is None else condition.astype(jnp.int32) for _, _, condition in links)
    pl.semaphore_wait(barrier, peers)


PATHS = ("zxy", "zyx", "xzy", "yzx")


class Link:
    def __init__(self, copy, sends=None, receives=None):
        self.copy, self.sends, self.receives = copy, sends, receives

    @staticmethod
    def when(condition, run):
        if condition is None:
            run()
        else:
            pl.when(condition)(run)

    def start(self):
        self.when(self.sends, lambda: self.copy.start())

    def wait_send(self):
        self.when(self.sends, lambda: self.copy.wait_send())

    def wait_recv(self):
        self.when(self.receives, lambda: self.copy.wait_recv())


class Pool:
    def __init__(self, array, count):
        self.array, self.free, self.users = array, list(range(count)), []

    def take(self, user):
        if not self.free:
            self.users[0].release()
        self.users.append(user)
        return self.free.pop(0)

    def give(self, user, at):
        self.users.remove(user)
        self.free.append(at)

    def drain(self):
        while self.users:
            self.users[0].release()


class PooledLink(Link):
    def __init__(self, make, pool, sends=None, receives=None):
        self.make, self.pool, self.sends, self.receives = make, pool, sends, receives
        self.at = None

    def start(self):
        self.at = self.pool.take(self)
        copy = self.make(self.pool.array.at[self.at])
        self.when(self.sends, lambda: copy.start())

    def release(self):
        copy = self.make(self.pool.array.at[self.at])
        self.when(self.sends, lambda: copy.wait_send())
        self.pool.give(self, self.at)

    def wait_recv(self):
        copy = self.make(self.pool.array.at[0])
        self.when(self.receives, lambda: copy.wait_recv())


class PooledCopy:
    def __init__(self, pool, source, target):
        self.pool, self.done = pool, False
        self.at = pool.take(self)
        self.copy = pltpu.make_async_copy(source, target, pool.array.at[self.at])
        self.copy.start()

    def wait(self):
        if not self.done:
            self.copy.wait()
            self.done = True
            self.pool.give(self, self.at)

    release = wait


class Exchange:
    def __init__(self, place, pool, receive):
        self.place, self.pool, self.receive, self.count = place, pool, receive, 0

    def slot(self):
        self.count += 1
        return self.count - 1

    def link(self, source, target, dim, there, sends=None, receives=None, slot=None):
        slot = self.slot() if slot is None else slot
        device = self.place.device(dim, there)

        def make(send):
            return pltpu.make_async_remote_copy(
                source, target, send, self.receive.at[slot], device_id=device, device_id_type=MESH
            )

        return PooledLink(make, self.pool, sends, receives)


def pick(held, place, **fixed):
    return tuple(fixed.get(dim, ALL if dim in held else place.at(dim)) for dim in "yczx")


def gather_steps(place, blocks, path, sems):
    steps, slot, held = [], 0, ""
    for dim in path + "c":
        here, size = place.at(dim), place.size(dim)
        if size == 2:
            there = 1 - here
            index = pick(held, place)
            copy = pltpu.make_async_remote_copy(
                blocks(index), blocks(index), sems[0].at[slot], sems[1].at[slot],
                device_id=place.device(dim, there), device_id_type=MESH,
            )
            steps.append([Link(copy)])
            slot += 1
        else:
            for hop in range(1, size):
                links = []
                for way in (1, -1):
                    origin = here - way * (hop - 1)
                    there = here + way
                    source = here - way * hop
                    index = pick(held, place, **{dim: jnp.clip(origin, 0, size - 1)})
                    copy = pltpu.make_async_remote_copy(
                        blocks(index), blocks(index), sems[0].at[slot], sems[1].at[slot],
                        device_id=place.device(dim, jnp.clip(there, 0, size - 1)), device_id_type=MESH,
                    )
                    sends = (origin >= 0) & (origin < size) & (there >= 0) & (there < size)
                    links.append(Link(copy, sends, (source >= 0) & (source < size)))
                    slot += 1
                steps.append(links)
        held += dim
    return steps


def slot_count(sizes):
    ny, nz = sizes
    return 2 + (1 if ny == 2 else 2 * (ny - 1)) + (1 if nz == 2 else 2 * (nz - 1))


def run_steps(plans, lag):
    rounds = max(lag[i] + len(plan) for i, plan in enumerate(plans)) + 1
    for now in range(rounds):
        for offset, plan in zip(lag, plans):
            at = now - offset
            if 1 <= at <= len(plan):
                for link in plan[at - 1]:
                    link.wait_recv()
            if 0 <= at < len(plan):
                for link in plan[at]:
                    link.start()
    for plan in plans:
        for links in plan:
            for link in links:
                link.wait_send()


def gather_kernel(sizes, *refs):
    shards, wholes = refs[:11], refs[11:22]
    own_sem, send_sem, recv_sem = refs[22:]
    place = Place(sizes)
    own = (place.y, place.c, place.z, place.x)
    owns = [
        pltpu.make_async_copy(shard, whole.at[own], own_sem.at[i])
        for i, (shard, whole) in enumerate(zip(shards, wholes))
    ]
    for copy in owns:
        copy.start()
    neighbour_barrier(place)
    views = [lambda index, ref=ref: ref.at[index] for ref in wholes[:9]]
    width = wholes[8].shape[-1]
    for q in range(4):
        views.append(
            lambda index, q=q: wholes[9].at[index + (ALL, pl.ds(q * width, width))]
        )
    for q in range(4):
        views.append(lambda index, q=q: wholes[10].at[index + (q,)])
    plans, lag = [], []
    for i, view in enumerate(views):
        path = PATHS[0] if i == 0 else PATHS[(i - 1) % 4]
        plans.append(gather_steps(place, view, path, (send_sem.at[i], recv_sem.at[i])))
        lag.append(0 if i == 0 else 3 * ((i - 1) // 4))
    for copy in owns:
        copy.wait()
    run_steps(plans, lag)


def gather_weights(sizes, table, gains, squares, inner, outer):
    ny, nz = sizes
    grid = (ny, 2, nz, 2)
    part, width = squares[0].shape
    small = jnp.zeros((16, 128), table.dtype)
    small = small.at[: table.shape[0], :part].set(table)
    for i, gain in enumerate(gains):
        small = small.at[table.shape[0] + i, :part].set(gain)
    shards = (small,) + tuple(squares) + (inner, outer.reshape(4, part, width))
    anywhere = pl.BlockSpec(memory_space=pl.ANY)
    slots = slot_count(sizes)
    wholes = pl.pallas_call(
        functools.partial(gather_kernel, sizes),
        out_shape=[jax.ShapeDtypeStruct(grid + s.shape, s.dtype) for s in shards],
        in_specs=[anywhere] * 11,
        out_specs=[anywhere] * 11,
        scratch_shapes=[
            pltpu.SemaphoreType.DMA((11,)),
            pltpu.SemaphoreType.DMA((17, slots)),
            pltpu.SemaphoreType.DMA((17, slots)),
        ],
        compiler_params=pltpu.CompilerParams(collective_id=0, has_side_effects=True),
    )(*shards)
    count = ny * nz * 4
    tiny = wholes[0].reshape(count, 16, 128)[:, :, :part].transpose(1, 0, 2).reshape(16, count * part)
    rows = table.shape[0]
    return (
        (tiny[rows], tiny[rows + 1], tiny[rows + 2], tiny[:rows])
        + tuple(w.reshape(count * part, width) for w in wholes[1:9])
        + (wholes[9].reshape(count * part, 4 * width), wholes[10].reshape(4 * count * part, width))
    )


class Reduce:
    def __init__(self, place, path, source, total, core_in, boxes, out, sems):
        self.place, self.path, self.source, self.total = place, path, source, total
        self.core_in, self.boxes, self.out, self.sems = core_in, boxes, out, sems
        self.slot = 0
        self.sent = []

    def copy(self, source, target, dim, there):
        slot = self.slot
        self.slot += 1
        return pltpu.make_async_remote_copy(
            source, target, self.sems[0].at[slot], self.sems[1].at[slot],
            device_id=self.place.device(dim, there), device_id_type=MESH,
        )

    def index(self, fixed):
        return tuple(fixed.get(dim, ALL) for dim in "yzx")

    def add(self, target, box):
        shape = box.shape[:-2]
        count = 1
        for size in shape:
            count *= size
        free = [i for i, entry in enumerate(target) if entry is ALL]

        def body(n, _):
            spots, rest = [], n
            for size in reversed(shape):
                spots.append(lax.rem(rest, size))
                rest = lax.div(rest, size)
            spots = spots[::-1]
            full = list(target)
            for place_at, spot in zip(free, spots):
                full[place_at] = spot
            mine = self.total[tuple(full)].astype(jnp.float32)
            got = box[tuple(spots)].astype(jnp.float32)
            self.total[tuple(full)] = (mine + got).astype(jnp.bfloat16)
            return 0

        if count == 1:
            body(0, 0)
        else:
            lax.fori_loop(0, count, body, 0)

    def steps(self):
        place, listing = self.place, []
        own = pltpu.make_async_copy(self.source(place.c), self.total, self.sems[2])
        core = self.copy(self.source(1 - place.c), self.core_in, "c", 1 - place.c)

        def start():
            own.start()
            core.start()

        def finish():
            own.wait()
            core.wait_recv()
            self.add((ALL, ALL, ALL), self.core_in)

        self.sent.append(Link(core))
        listing.append((start, finish))
        fixed, box = {}, 0
        for dim in self.path:
            here, size = place.at(dim), place.size(dim)
            if size == 2:
                target = self.index({**fixed, dim: 1 - here})
                link = Link(self.copy(self.total.at[target], self.boxes[box], dim, 1 - here))
                self.sent.append(link)
                listing.append(self.pair([link], [(self.index({**fixed, dim: here}), box, None)]))
                box += 1
            else:
                for hop in range(size - 1, 0, -1):
                    links, adds = [], []
                    for way in (1, -1):
                        there = here - way
                        goal = here - way * hop
                        sends = (goal >= 0) & (goal < size)
                        source = here + way
                        got = source - way * hop
                        receives = (source >= 0) & (source < size) & (got >= 0) & (got < size)
                        target = self.index({**fixed, dim: jnp.clip(goal, 0, size - 1)})
                        copy = self.copy(
                            self.total.at[target], self.boxes[box], dim, jnp.clip(there, 0, size - 1)
                        )
                        link = Link(copy, sends, receives)
                        self.sent.append(link)
                        links.append(link)
                        adds.append((self.index({**fixed, dim: jnp.clip(got, 0, size - 1)}), box, receives))
                        box += 1
                    listing.append(self.pair(links, adds))
            fixed = {**fixed, dim: here}
        return listing

    def pair(self, links, adds):
        def start():
            for link in links:
                link.start()

        def finish():
            for link in links:
                link.wait_recv()
            for target, box, condition in adds:
                Link.when(condition, functools.partial(self.add, target, self.boxes[box]))

        return start, finish

    def close(self):
        own = (self.place.y, self.place.z, self.place.x)
        self.out(self.total[own].astype(jnp.float32))
        for link in self.sent:
            link.wait_send()


def box_shapes(sizes, path):
    ny, nz = sizes
    size = {"y": ny, "z": nz, "x": 2}
    left, shapes = "yzx", []
    for dim in path:
        left = left.replace(dim, "")
        lead = tuple(size[d] for d in left)
        shapes += [lead] * (1 if size[dim] == 2 else 2 * (size[dim] - 1))
    return shapes


BACK_PATHS = tuple(path[::-1] for path in PATHS)


def reduce_kernel(sizes, box_counts, *refs):
    sources, small_in = refs[:10], refs[10]
    outs, small_out = refs[11:21], refs[21]
    totals, core_boxes = refs[22], refs[23]
    at = 24
    boxes = []
    for count in box_counts:
        boxes.append(refs[at : at + count])
        at += count
    small_box, own_sem, send_sem, recv_sem, small_send, small_recv = refs[at:]
    place = Place(sizes)
    neighbour_barrier(place, far=True)
    width = outs[0].shape[-1]

    def square(ref):
        return lambda core: ref.at[:, core]

    def inner(q):
        return lambda core: sources[8].at[:, core, :, :, :, pl.ds(q * width, width)]

    def outer(q):
        return lambda core: sources[9].at[:, core, :, :, q]

    views = [inner(q) for q in range(4)] + [outer(q) for q in range(4)]
    views += [square(sources[i]) for i in (4, 5, 6, 7, 0, 1, 2, 3)]

    def store_square(i):
        def run(value):
            outs[i][...] = value

        return run

    def store_inner(q):
        def run(value):
            outs[8][:, q * width : (q + 1) * width] = value

        return run

    def store_outer(q):
        def run(value):
            outs[9][q] = value

        return run

    stores = [store_inner(q) for q in range(4)] + [store_outer(q) for q in range(4)]
    stores += [store_square(i) for i in (4, 5, 6, 7, 0, 1, 2, 3)]
    plans, lag = [], []
    reduces = []
    for m in range(16):
        group, kind = m // 4, m % 4
        reduce = Reduce(
            place, BACK_PATHS[kind], views[m], totals.at[m], core_boxes.at[m],
            [box.at[group] for box in boxes[kind]], stores[m],
            (send_sem.at[m], recv_sem.at[m], own_sem.at[m]),
        )
        reduces.append(reduce)
        plans.append(reduce.steps())
        lag.append(3 * group)
    small_out[...] = small_in[...]
    small = []
    moves = [("c", 1 - place.c), ("x", 1 - place.x), ("y", None), ("z", None)]
    for dim, there in moves:
        size, here, reach = place.size(dim), place.at(dim), 1
        while reach < size:
            partner = here + reach - 2 * reach * lax.rem(lax.div(here, reach), 2)
            small.append((dim, partner))
            reach *= 2
    rounds = max(max(lag[i] + len(plan) for i, plan in enumerate(plans)) + 1, len(small) + 1)
    copies = []
    for now in range(rounds):
        for offset, plan in zip(lag, plans):
            step = now - offset
            if 1 <= step <= len(plan):
                plan[step - 1][1]()
            if 0 <= step < len(plan):
                plan[step][0]()
        if 1 <= now <= len(small):
            copies[-1].wait()
            small_out[...] += small_box[now - 1]
        if now < len(small):
            dim, partner = small[now]
            copies.append(
                pltpu.make_async_remote_copy(
                    small_out, small_box.at[now], small_send.at[now], small_recv.at[now],
                    device_id=place.device(dim, partner), device_id_type=MESH,
                )
            )
            copies[-1].start()
    for reduce in reduces:
        reduce.close()


def reduce_grads(sizes, language, bucket, gains, squares, inner, outer):
    ny, nz = sizes
    grid = (ny, 2, nz, 2)
    count = ny * nz * 4
    width = squares[0].shape[1]
    part = squares[0].shape[0] // count
    langs = language.shape[0]
    flat = jnp.zeros((width,), jnp.float32).at[: bucket.size].set(bucket.reshape(-1))
    small = jnp.concatenate(
        [language] + [g.reshape(1, width) for g in gains] + [flat[None], jnp.zeros((4, width), jnp.float32)], axis=0
    )
    sources = [to_low(s).reshape(grid + (part, width)) for s in squares]
    sources += [
        to_low(inner).reshape(grid + (part, 4 * width)),
        to_low(outer).reshape(grid + (4, part, width)),
    ]
    anywhere = pl.BlockSpec(memory_space=pl.ANY)
    vmem = pl.BlockSpec(memory_space=pltpu.VMEM)
    shapes = [(part, width)] * 8 + [(part, 4 * width), (4, part, width), small.shape]
    lead = [box_shapes(sizes, path) for path in BACK_PATHS]
    slots = slot_count(sizes)
    hops = (ny * nz * 4).bit_length() - 1
    outs = pl.pallas_call(
        functools.partial(reduce_kernel, sizes, tuple(len(s) for s in lead)),
        out_shape=[jax.ShapeDtypeStruct(s, jnp.float32) for s in shapes],
        in_specs=[anywhere] * 10 + [vmem],
        out_specs=[vmem] * 11,
        scratch_shapes=[
            pltpu.VMEM((16, ny, nz, 2, part, width), jnp.bfloat16),
            pltpu.VMEM((16, ny, nz, 2, part, width), jnp.bfloat16),
        ]
        + [pltpu.VMEM((4,) + s + (part, width), jnp.bfloat16) for one in lead for s in one]
        + [
            pltpu.VMEM((hops,) + small.shape, jnp.float32),
            pltpu.SemaphoreType.DMA((16,)),
            pltpu.SemaphoreType.DMA((16, slots)),
            pltpu.SemaphoreType.DMA((16, slots)),
            pltpu.SemaphoreType.DMA((hops,)),
            pltpu.SemaphoreType.DMA((hops,)),
        ],
        compiler_params=pltpu.CompilerParams(
            collective_id=1, has_side_effects=True, vmem_limit_bytes=60 * 1024 * 1024
        ),
    )(*sources, small)
    start = (lax.axis_index("dp") * nz * 2 + lax.axis_index("fsdp")) * part
    total = outs[10]
    mine = lax.dynamic_slice(total, (0, start), (langs + 3, part))
    return (
        mine[:langs],
        total[langs + 3, : bucket.size].reshape(bucket.shape),
        mine[langs], mine[langs + 1], mine[langs + 2],
        outs[:8], outs[8], outs[9].reshape(4 * part, width),
    )


FORWARD_PATHS = (
    "zxy", "yzx", "zxy", "zyx", "zyx", "xzy", "zxy", "zxy", "zyx", "xyz", "zyx", "yxz", "zxy", "zxy", "zyx",
    "zyx", "xyz",
)
FORWARD_ORDER = (
    2, 11, 0, 9, 3, 1, 5, 16, 4, 2, 9, 3, 11, 0, 6, 16, 2, 5, 3, 1, 2, "b0", 4, 7, 0, 3, 1, 5, 0, 4, 13, 8, 6,
    2, "b1", 7, 3, 1, 4, 12, 6, 0, 10, "b2", 5, 1, 14, 6, 8, 3, 7, 2, 0, 10, 0, 1, 14, 12, 5, 9, 8, 2, 3, 13, 7,
    "b3", 4, 5, 12, "open", 6, 11, "k", 1, "q", "v", 5, 8, 15, 7, "sa0", 12, 10, 4, "sa1", 9, 6, "sa2", 8,
    "sa3", 14, 4, "se0", "se1", 9, 13, 10, 6, 7, 16, "K", "cq", 14, 15, 7, 12, "V", 11, "ca0", 8, 9, 10, 13,
    "ca1", 15, "ca2", "ca3", 10, 11, 16, 9, 8, 15, 14, "ce0", "ce1", "in0", 13, 12, "og0", 11, 10, "in1", 16,
    12, 15, "og1", 14, 13, 11, "in2", 16, "in3", 15, 14, "og3", 13, "og2", 16, 15,
)
BACKWARD_PATHS = (
    "xzy", "yzx", "yxz", "xyz", "xzy", "xyz", "yxz", "yzx", "yzx", "yxz", "xyz", "xzy", "xyz", "xzy", "yzx",
    "yxz",
)
BACKWARD_ORDER = (
    3, "x0", 2, "in0", 0, 4, 3, "t0", 2, "x1", 0, "in1", 1, 3, "t1", "x2", 0, 1, 5, 4, "in2", 2, "t2", 6, "x3",
    3, "in3", 1, 0, "t3", 7, 4, 6, "n3", 5, "co", 1, "ccg", 2, 7, 0, "ca0", 6, "ca1", "ca2", "ca3", 4, 8, 7, 1,
    "ca4", "ca5", 5, "cv", 11, "cq", 7, 9, "ck", 10, 11, 4, 8, "n2a", 1, 9, "n2", 10, 6, 3, "so", 5, 8, 2,
    "scg", 12, 0, 11, "sa0", 9, 5, "sa1", 6, 10, 2, 8, "sa2", 3, 4, "k", 7, 14, "v", 11, 15, "cp0", "q", 3, 14,
    12, 13, 5, 2, "cp1", 9, 10, 15, 1, "bk0", 13, 11, "bk1", 9, 4, 0, 14, 7, "bk2", 10, 12, 6, "cp2", "cl1", 13,
    "bk3", 15, 14, "bk4", 8, "bk5", 16, 12, "h0", 5, 7, 16, 6, 13, "h1", 9, "h2", 12, "h3", 15, 16, 14, "e0k",
    13, 9, "e0v", 16, 15, 10, 11, 12, "e1k", 13, 14, 8, 11, 16, 15, "e1v", 13, 8, 10, 12, 15, 14, 16,
)


LOW = jnp.bfloat16
FULL = jnp.float32
PAIR = 2 * HEAD


def nt_dot(left, right):
    return lax.dot_general(left, right, (((1,), (1,)), ((), ())), preferred_element_type=FULL)


def tn_dot(left, right):
    return lax.dot_general(left, right, (((0,), (0,)), ((), ())), preferred_element_type=FULL)


def flat(ref, *suffix):
    value = ref[(ALL,) * (len(ref.shape) - 1) + suffix] if suffix else ref[...]
    rows = 1
    for size in value.shape[:-1]:
        rows *= size
    return value.reshape(rows, value.shape[-1])


def each(count, body):
    def run(i, _):
        body(pl.ds(pl.multiple_of(i * 128, 128), 128))
        return 0

    lax.fori_loop(0, count, run, 0)


def unit_rows(hidden):
    return hidden * lax.rsqrt(jnp.mean(hidden * hidden, axis=-1, keepdims=True) + EPSILON)


def spread_small(tiny, table):
    part = table.shape[1] // (tiny.shape[0] * tiny.shape[2] * 4)
    table[...] = jnp.zeros_like(table)
    lane = lax.broadcasted_iota(jnp.int32, (16, 128), 1)
    at = 0
    for y in range(tiny.shape[0]):
        for core in range(2):
            for z in range(tiny.shape[2]):
                for x in range(2):
                    slab = jnp.where(lane < part, tiny[y, core, z, x], 0.0)
                    base, shift = at // 128 * 128, at % 128
                    if shift:
                        slab = pltpu.roll(slab, shift, 1)
                    if shift + part <= 128:
                        table[:, base : base + 128] += slab
                    else:
                        table[:, base : base + 128] += jnp.where(lane >= part, slab, 0.0)
                        table[:, base + 128 : base + 256] += jnp.where(lane < part, slab, 0.0)
                    at += part


def build_bias(ids, values, bias, heads):
    keys, queries = bias.shape[1:]
    rows = 64

    def block(n, _):
        at = pl.ds(pl.multiple_of(n * rows, rows), rows)
        bucket = ids[at, :]
        bits = [lax.bitwise_and(bucket, 1 << b) != 0 for b in range(5)]
        key = n * rows + lax.broadcasted_iota(jnp.int32, (rows, queries), 0)
        query = lax.broadcasted_iota(jnp.int32, (rows, queries), 1)
        hidden = key > query

        def head(h, _):
            level = [values[16 + h, c] for c in range(32)]
            for bit in bits:
                level = [jnp.where(bit, level[i + 1], level[i]) for i in range(0, len(level), 2)]
            bias[h, at, :] = jnp.where(hidden, NEGATIVE, level[0]).astype(LOW)
            return 0

        return lax.fori_loop(*heads, head, 0)

    lax.fori_loop(0, keys // rows, block, 0)


def head_pair(value):
    lane = lax.broadcasted_iota(jnp.int32, value.shape, 1)
    zero = jnp.zeros_like(value)
    return jnp.concatenate([jnp.where(lane < HEAD, value, zero), jnp.where(lane < HEAD, zero, value)], axis=0)


def pairs_forward(items):
    scores = [nt_dot(keys, head_pair(queries)) for queries, keys, _, _ in items]
    scores = [s if item[3] is None else s + item[3] for s, item in zip(scores, items)]
    grown = [jnp.exp(s - jnp.max(s, axis=0, keepdims=True)) for s in scores]
    rows = [1.0 / jnp.sum(g, axis=0, keepdims=True) for g in grown]
    weights = [g.astype(LOW) for g in grown]
    results = []
    for (queries, _, values, _), low, row in zip(items, weights, rows):
        count = queries.shape[0]
        lane = lax.broadcasted_iota(jnp.int32, values.shape, 1)
        one = jnp.ones_like(values)
        first = tn_dot(low[:, :count], jnp.where(lane < HEAD, values, one))
        second = tn_dot(low[:, count:], jnp.where(lane < HEAD, one, values))
        lane = lax.broadcasted_iota(jnp.int32, first.shape, 1)
        inverse = 1.0 / pltpu.roll(jnp.where(lane < HEAD, second, first), HEAD, 1)
        results.append((jnp.where(lane < HEAD, first, second) * inverse, inverse, low, row))
    return results


def gelu_parts(u):
    a, b = 0.7978845608028654, 0.044715
    square = u * u
    t = jnp.tanh(a * u * (1.0 + b * square))
    half = 0.5 * (1.0 + t)
    slope = half + 0.5 * u * (1.0 - t * t) * (a * (1.0 + 3.0 * b * square))
    return u * half, slope


def gather_plans(place, wholes, small, exchange):
    views = [lambda index, ref=ref: ref.at[index] for ref in [small] + list(wholes[:8])]
    width = wholes[0].shape[-1]
    for q in range(4):
        views.append(lambda index, q=q: wholes[8].at[index + (ALL, pl.ds(q * width, width))])
    for q in range(4):
        views.append(lambda index, q=q: wholes[9].at[index + (q,)])
    return [gather_early(place, view, path, exchange) for view, path in zip(views, FORWARD_PATHS)]


def gather_early(place, blocks, path, exchange):
    steps = []
    at = {dim: place.at(dim) for dim in "yczx"}

    def link(dim, there, where, sends=None, receives=None, slot=None):
        view = blocks(tuple(where.get(d, at[d]) for d in "yczx"))
        return exchange.link(view, view, dim, there, sends, receives, slot)

    def swap(dim, where):
        return link(dim, 1 - at[dim], where)

    def slots(hop):
        first = exchange.slot()
        return first, first if 2 * hop >= place.nz else exchange.slot()

    def hops(hop, where):
        here, size, links = at["z"], place.nz, []
        for way, slot in zip((1, -1), slots(hop)):
            origin, there, source = here - way * (hop - 1), here + way, here - way * hop
            sends = (origin >= 0) & (origin < size) & (there >= 0) & (there < size)
            receives = (source >= 0) & (source < size)
            spot = {**where, "z": jnp.clip(origin, 0, size - 1)}
            links.append(link("z", jnp.clip(there, 0, size - 1), spot, sends, receives, slot))
        return links

    def swap_arrived(dim, hop, where):
        here, size, links = at["z"], place.nz, []
        for way, slot in zip((1, -1), slots(hop)):
            source = here - way * hop
            here_now = (source >= 0) & (source < size)
            spot = {**where, "z": jnp.clip(source, 0, size - 1)}
            links.append(link(dim, 1 - at[dim], spot, here_now, here_now, slot))
        return links

    last = path[2]
    if last == "z":
        first, second = path[0], path[1]
        steps = [[swap(first, {})], [swap(second, {first: ALL})]]
        steps += [hops(hop, {first: ALL, second: ALL}) for hop in range(1, place.nz)]
        steps.append([swap("c", {"y": ALL, "z": ALL, "x": ALL})])
        return steps
    if path[0] == "z":
        first = path[1]
        steps = [hops(hop, {}) for hop in range(1, place.nz)]
        steps.append([swap(first, {"z": ALL}), swap(last, {"z": ALL})])
        steps.append([swap(last, {"z": ALL, first: 1 - at[first]})])
    else:
        first = path[0]
        steps.append([swap(first, {})])
        steps.append(hops(1, {first: ALL}) + [swap(last, {first: ALL})])
        for hop in range(2, place.nz):
            steps.append(hops(hop, {first: ALL}) + swap_arrived(last, hop - 1, {first: ALL}))
        steps.append(swap_arrived(last, place.nz - 1, {first: ALL}))
    steps[-1].append(swap("c", {"z": ALL, first: ALL}))
    steps.append([swap("c", {"z": ALL, first: ALL, last: 1 - at[last]})])
    return steps


def run_order(order, plans, tasks, done):
    at = [0] * len(plans)
    for entry in order:
        if isinstance(entry, str):
            tasks[entry]()
            continue
        step, plan = at[entry], plans[entry]
        at[entry] += 1
        if step >= 1:
            for link in plan[step - 1]:
                link.wait_recv()
        if step < len(plan):
            for link in plan[step]:
                link.start()
        else:
            done(entry)


SAVED = (
    "first_norm", "queries", "keys", "values", "self_context", "second_norm", "cross_queries",
    "source_keys", "source_values", "cross_context", "third_norm", "activated", "slope",
    "start", "mid", "late", "self_inverse", "cross_inverse", "self_rows", "cross_rows", "table",
)


def saved_shapes(tokens, sources, width, length):
    low, full = LOW, FULL
    row = (tokens, width)
    pairs = tokens // length * (width // PAIR)
    shapes = {name: (row, low) for name in SAVED}
    shapes["source_keys"] = shapes["source_values"] = ((2, sources // 2, width), low)
    shapes["activated"] = shapes["slope"] = ((4,) + row, low)
    for name in ("start", "mid", "late", "self_inverse", "cross_inverse"):
        shapes[name] = (row, full)
    shapes["self_rows"] = shapes["cross_rows"] = ((pairs, 1, 2 * length), full)
    shapes["table"] = ((16, width), full)
    return shapes


def forward_kernel(sizes, *refs):
    n = len(SAVED)
    small_shard, shards = refs[0], refs[1:11]
    hidden_in, upstream_in, encoder_in, languages, sources, ids, slab_values = refs[11:18]
    outer_grads, whole_outs = refs[18], refs[19:29]
    self_weights, cross_weights = refs[29:31]
    saved_outs = dict(zip(SAVED, refs[31 : 31 + n]))
    at = 31 + n
    tiny, wholes = refs[at], refs[at + 1 : at + 11]
    at += 11
    v = dict(zip(SAVED, refs[at : at + n]))
    at += n
    bias, stage, outer_blocks, hidden, upstream, encoder, ids_across = refs[at : at + 7]
    send_sem, recv_sem, copy_sem = refs[at + 7 :]
    tokens, width = hidden.shape
    length = ids.shape[0]
    per_seq = width // PAIR
    seqs = tokens // length
    enc_length = encoder.shape[0] // 2
    blocks = tokens // 128

    place = Place(sizes)
    own = (place.y, place.c, place.z, place.x)
    moving = Pool(copy_sem, copy_sem.shape[0])
    sending = Pool(send_sem, send_sem.shape[0])
    owns = [
        PooledCopy(moving, shard, whole.at[own])
        for shard, whole in zip((small_shard.at[pl.ds(0, 16)],) + shards, (tiny,) + wholes)
    ]
    inputs = [
        PooledCopy(moving, source, target)
        for source, target in ((hidden_in, hidden), (encoder_in, encoder), (upstream_in, upstream))
    ]
    neighbour_barrier(place)
    plans = gather_plans(place, wholes, tiny, Exchange(place, sending, recv_sem))
    for copy in owns:
        copy.wait()

    def keep(name):
        PooledCopy(moving, v[name], saved_outs[name])

    def keep_whole(m):
        if m == 0:
            return
        if m < 9:
            source, target = wholes[m - 1], whole_outs[m - 1]
        elif m < 13:
            index = (ALL,) * 5 + (pl.ds((m - 9) * width, width),)
            source, target = wholes[8].at[index], whole_outs[8].at[index]
        else:
            index = (ALL,) * 4 + (m - 13,)
            source, target = wholes[9].at[index], whole_outs[9].at[index]
        PooledCopy(moving, source, target)

    def opening():
        inputs.pop(0).wait()
        spread_small(tiny, v["table"])
        for s in range(seqs):
            row = jnp.zeros((1, width), FULL)
            for l in range(8):
                row = row + jnp.where(languages[s] == l, v["table"][l : l + 1, :], 0.0)

            def body(at):
                start = hidden[at, :].astype(FULL) + row
                v["start"][at, :] = start
                v["first_norm"][at, :] = (unit_rows(start) * v["table"][8:9, :]).astype(LOW)

            def run(i, _):
                body(pl.ds(pl.multiple_of(s * length + i * 128, 128), 128))
                return 0

            lax.fori_loop(0, length // 128, run, 0)
        keep("table")
        keep("start")
        keep("first_norm")

    def project(source, weight, target):
        target[...] = jnp.dot(source[...], flat(weight), preferred_element_type=FULL).astype(LOW)

    leaving = {}

    def attention(turn, queries, keys, values, context, inverse, rows, weights_out, seq, first, last, picked):
        row_at = pl.ds(seq * length, length)
        key_rows = length if picked is None else enc_length
        items = []
        for p in range(first, last):
            lanes = pl.ds(p * PAIR, PAIR)
            if picked is not None:
                items.append((queries[row_at, lanes], keys[picked, :, lanes], values[picked, :, lanes], None))
            else:
                offset = jnp.concatenate([bias[2 * p], bias[2 * p + 1]], axis=1).astype(FULL)
                items.append((queries[row_at, lanes], keys[row_at, lanes], values[row_at, lanes], offset))
        for n, (out, total, low, row) in enumerate(pairs_forward(items)):
            lanes = pl.ds((first + n) * PAIR, PAIR)
            index = seq * per_seq + first + n
            slot = turn % 2 * (last - first) + n
            if slot in leaving:
                leaving[slot].wait()
            part = stage.at[slot, pl.ds(0, key_rows)]
            part[...] = low
            rows[index] = row
            context[row_at, lanes] = out.astype(LOW)
            inverse[row_at, lanes] = total
            leaving[slot] = PooledCopy(moving, part, weights_out.at[index])

    def residual(half, context, weight, before, after, gain_row, norm):
        at = pl.ds(half * (tokens // 2), tokens // 2)
        state = before[at, :] + jnp.dot(context[at, :], flat(weight), preferred_element_type=FULL)
        after[at, :] = state
        norm[at, :] = (unit_rows(state) * v["table"][gain_row : gain_row + 1, :]).astype(LOW)

    def self_projection(i, name):
        project(v["first_norm"], wholes[i], v[name])
        keep(name)

    def self_attention(turn, s, first, last):
        attention(
            turn, v["queries"], v["keys"], v["values"], v["self_context"], v["self_inverse"], v["self_rows"],
            self_weights, s, first, last, None,
        )

    def self_end(half):
        if half == 0:
            for name in ("self_context", "self_inverse", "self_rows"):
                keep(name)
        residual(half, v["self_context"], wholes[3], v["start"], v["mid"], 9, v["second_norm"])
        if half:
            keep("mid")
            keep("second_norm")

    def cross_source(i, name):
        if len(inputs) == 2:
            inputs.pop(0).wait()
        for half in range(2):
            v[name][half] = jnp.dot(
                encoder[pl.ds(half * enc_length, enc_length), :], flat(wholes[i]), preferred_element_type=FULL
            ).astype(LOW)
        keep(name)

    def cross_projection():
        project(v["second_norm"], wholes[4], v["cross_queries"])
        keep("cross_queries")

    def cross_attention(turn, s, first, last):
        attention(
            turn, v["cross_queries"], v["source_keys"], v["source_values"], v["cross_context"], v["cross_inverse"],
            v["cross_rows"], cross_weights, s, first, last, sources[s],
        )

    def cross_end(half):
        if half == 0:
            for name in ("cross_context", "cross_inverse", "cross_rows"):
                keep(name)
        residual(half, v["cross_context"], wholes[7], v["mid"], v["late"], 10, v["third_norm"])
        if half:
            keep("late")
            keep("third_norm")

    def feed_inner(q):
        weight = flat(wholes[8], pl.ds(q * width, width))
        for half in range(2):
            at = pl.ds(half * tokens // 2, tokens // 2)
            expanded = jnp.dot(v["third_norm"][at, :], weight, preferred_element_type=FULL)
            value, slope = gelu_parts(expanded)
            v["activated"][q, at, :] = value.astype(LOW)
            v["slope"][q, at, :] = slope.astype(LOW)
        for name in ("activated", "slope"):
            PooledCopy(moving, v[name].at[q], saved_outs[name].at[q])

    def bias_values(turn):
        if turn == 0:
            ids_across[...] = ids[...].astype(FULL).T.astype(jnp.int32)
        build_bias(ids_across, slab_values, bias, (3 * turn, 3 * turn + 3))

    def outer_grad(q):
        if inputs:
            inputs.pop(0).wait()
        value = tn_dot(v["activated"][q], upstream[...])
        outer_blocks[q // 2, q % 2] = value.reshape(outer_blocks.shape[2:]).astype(LOW)
        chunk = q // 2, q % 2
        PooledCopy(moving, outer_blocks.at[chunk], outer_grads.at[chunk])

    tasks = {"open": opening, "cq": cross_projection}
    for half in range(2):
        tasks[f"se{half}"] = functools.partial(self_end, half)
        tasks[f"ce{half}"] = functools.partial(cross_end, half)
    for i, (task, name) in enumerate((("q", "queries"), ("k", "keys"), ("v", "values"))):
        tasks[task] = functools.partial(self_projection, i, name)
    for i in range(4):
        first = per_seq // 2 * (i % 2)
        tasks[f"sa{i}"] = functools.partial(self_attention, i, i // 2, first, first + per_seq // 2)
        tasks[f"ca{i}"] = functools.partial(cross_attention, i, i // 2, first, first + per_seq // 2)
        tasks[f"in{i}"] = functools.partial(feed_inner, i)
        tasks[f"b{i}"] = functools.partial(bias_values, i)
        tasks[f"og{i}"] = functools.partial(outer_grad, i)
    tasks["K"] = functools.partial(cross_source, 5, "source_keys")
    tasks["V"] = functools.partial(cross_source, 6, "source_values")
    run_order(FORWARD_ORDER, plans, tasks, keep_whole)
    sending.drain()
    moving.drain()


RECEIVES = {"xyz": 7, "yxz": 7, "zxy": 9, "zyx": 9, "xzy": 12, "yzx": 12}


def small_slab(table, gains, bucket_table):
    part = table.shape[1]
    own = jnp.concatenate([table] + [g.reshape(1, part) for g in gains], axis=0).astype(FULL)
    buckets = bucket_table.T.astype(FULL)
    own = jnp.pad(own, ((0, 32 - own.shape[0]), (0, 128 - part)))
    heads, count = buckets.shape
    return own + jnp.pad(buckets, ((16, 16 - heads), (0, 128 - count)))


def forward(
    sizes, hidden_in, output_grad, encoder_states, language_ids, source_index, bucket_ids, language_table, bucket_table, gains,
    squares, inner, outer,
):
    ny, nz = sizes
    grid = (ny, 2, nz, 2)
    part, width = squares[0].shape
    tokens = hidden_in.shape[0]
    length = bucket_ids.shape[0]
    encoder = encoder_states.reshape(-1, width)
    enc_length = encoder_states.shape[1]
    slab = small_slab(language_table, gains, bucket_table)
    shards = [slab] + list(squares) + [inner, outer.reshape(4, part, width)]
    wholes = [jax.ShapeDtypeStruct(grid + s.shape, s.dtype) for s in shards]
    wholes[0] = jax.ShapeDtypeStruct(grid + (16, 128), FULL)
    shapes = saved_shapes(tokens, encoder.shape[0], width, length)
    pairs = tokens // length * (width // PAIR)
    anywhere = pl.BlockSpec(memory_space=pl.ANY)
    vmem = pl.BlockSpec(memory_space=pltpu.VMEM)
    smem = pl.BlockSpec(memory_space=pltpu.SMEM)
    out_shape = [wholes[10]] + wholes[1:]
    out_shape += [jax.ShapeDtypeStruct((pairs, rows, 2 * length), LOW) for rows in (length, enc_length)]
    out_shape += [jax.ShapeDtypeStruct(*shapes[name]) for name in SAVED]
    outs = pl.pallas_call(
        functools.partial(forward_kernel, sizes),
        out_shape=out_shape,
        in_specs=[anywhere] * 11 + [anywhere] * 3 + [smem, smem, vmem, smem],
        out_specs=[anywhere] * len(out_shape),
        scratch_shapes=[pltpu.VMEM(w.shape, w.dtype) for w in wholes]
        + [pltpu.VMEM(*shapes[name]) for name in SAVED]
        + [
            pltpu.VMEM((H, length, length), LOW),
            pltpu.VMEM((6, enc_length, 2 * length), LOW),
            pltpu.VMEM(wholes[10].shape, LOW),
            pltpu.VMEM((tokens, width), LOW),
            pltpu.VMEM((tokens, width), LOW),
            pltpu.VMEM(encoder.shape, LOW),
            pltpu.VMEM((length, length), jnp.int32),
            pltpu.SemaphoreType.DMA((48,)),
            pltpu.SemaphoreType.DMA((sum(RECEIVES[path] for path in FORWARD_PATHS),)),
            pltpu.SemaphoreType.DMA((28,)),
        ],
        compiler_params=pltpu.CompilerParams(
            collective_id=2, has_side_effects=True, vmem_limit_bytes=62 * 1024 * 1024
        ),
    )(
        *shards, hidden_in, output_grad, encoder, language_ids, source_index, bucket_ids, slab,
    )
    return outs


class Summed:
    def __init__(self, place, path, blocks, leaving, core_in, boxes, exchange):
        self.blocks, self.stages = blocks, []
        c = place.c
        core = exchange.link(leaving(1 - c), core_in, "c", 1 - c)
        self.stages.append(([core], [((ALL, c, ALL, ALL), core_in, None)]))
        self.box, self.boxes, self.exchange, self.place = 0, boxes, exchange, place
        first, last = path[0], path[2]
        fixed = {"c": c}
        if last == "z":
            second = path[1]
            self.stages.append(self.join(self.swap(first, {**fixed, second: 1 - place.at(second)})))
            fixed[first] = place.at(first)
            here = self.swap(first, {"c": c, second: place.at(second)})
            self.stages.append(self.join(self.swap(second, fixed), here))
            fixed[second] = place.at(second)
            for hop in range(place.nz - 1, 0, -1):
                self.stages.append(self.join(self.hops(hop, fixed)))
        else:
            after = {**fixed, first: place.at(first)}
            self.stages.append(self.join(self.swap_goals(first, place.nz - 1, fixed)))
            for hop in range(place.nz - 1, 1, -1):
                self.stages.append(self.join(self.hops(hop, after), self.swap_goals(first, hop - 1, fixed)))
            own = self.swap(first, {**fixed, "z": place.z})
            self.stages.append(self.join(self.hops(1, after), own))
            self.stages.append(self.join(self.swap(last, {**after, "z": place.z})))
        fixed = {"c": c, "y": place.y, "z": place.z, "x": place.x}
        self.own = self.index(fixed)

    def index(self, fixed):
        return tuple(fixed.get(dim, ALL) for dim in "yczx")

    @staticmethod
    def join(*parts):
        return [link for part in parts for link, _ in part], [add for part in parts for _, add in part]

    def next_box(self):
        self.box += 1
        return self.boxes[self.box - 1]

    def swap(self, dim, where):
        box, here = self.next_box(), self.place.at(dim)
        link = self.exchange.link(self.blocks(self.index({**where, dim: 1 - here})), box, dim, 1 - here)
        return [(link, (self.index({**where, dim: here}), box, None))]

    def swap_goals(self, dim, hop, where):
        pairs, here = [], self.place.at(dim)
        first = self.exchange.slot()
        second = first if 2 * hop >= self.place.nz else self.exchange.slot()
        for way, slot in ((1, first), (-1, second)):
            goal = self.place.z - way * hop
            there = (goal >= 0) & (goal < self.place.nz)
            spot = {**where, "z": jnp.clip(goal, 0, self.place.nz - 1)}
            box = self.next_box()
            source = self.blocks(self.index({**spot, dim: 1 - here}))
            link = self.exchange.link(source, box, dim, 1 - here, there, there, slot)
            pairs.append((link, (self.index({**spot, dim: here}), box, there)))
        return pairs

    def hops(self, hop, where):
        pairs, here, size = [], self.place.z, self.place.nz
        first = self.exchange.slot()
        second = first if 2 * hop > size + 1 else self.exchange.slot()
        for way, slot in ((1, first), (-1, second)):
            there, goal = here - way, here - way * hop
            sends = (goal >= 0) & (goal < size)
            source = here + way
            got = source - way * hop
            receives = (source >= 0) & (source < size) & (got >= 0) & (got < size)
            box = self.next_box()
            view = self.blocks(self.index({**where, "z": jnp.clip(goal, 0, size - 1)}))
            link = self.exchange.link(view, box, "z", jnp.clip(there, 0, size - 1), sends, receives, slot)
            pairs.append((link, (self.index({**where, "z": jnp.clip(got, 0, size - 1)}), box, receives)))
        return pairs

    def start(self, step):
        for link in self.stages[step][0]:
            link.start()

    def finish(self, step):
        links, adds = self.stages[step]
        for link in links:
            link.wait_recv()

        def add(target, box):
            view = self.blocks(target)
            view[...] = view[...] + box[...]

        for target, box, condition in adds:
            Link.when(condition, functools.partial(add, target, box))


def sum_boxes(sizes, path):
    size = {"y": sizes[0], "z": sizes[1], "x": 2}
    hops = 2 * (size["z"] - 1)
    if path[2] == "z":
        return [(size["z"],)] * 3 + [()] * hops, 9
    wide = (size[path[2]],)
    steps = [wide, wide]
    shapes = steps[:]
    for _ in range(size["z"] - 2):
        shapes += [wide] * 4
    return shapes + [wide] * 3 + [()], 12


def pairs_backward(items):
    stacked = [head_pair(item[4]) for item in items]
    prob_grads = [nt_dot(item[3], grads) for item, grads in zip(items, stacked)]
    value_parts = [jnp.dot(item[0], grads, preferred_element_type=FULL) for item, grads in zip(items, stacked)]
    scaled = [item[0].astype(FULL) * grads for item, grads in zip(items, prob_grads)]
    centres = [jnp.sum(s, axis=0, keepdims=True) * item[5] for s, item in zip(scaled, items)]
    score_grads = [(s - item[0].astype(FULL) * c).astype(LOW) for s, c, item in zip(scaled, centres, items)]
    key_parts = [jnp.dot(s, head_pair(item[1]), preferred_element_type=FULL) for s, item in zip(score_grads, items)]
    results = []
    for item, value_part, key_part, score_grad in zip(items, value_parts, key_parts, score_grads):
        count = item[1].shape[0]
        lane = lax.broadcasted_iota(jnp.int32, (count, PAIR), 1)
        first, second = tn_dot(score_grad[:, :count], item[2]), tn_dot(score_grad[:, count:], item[2])
        results.append((jnp.where(lane < HEAD, first, second), key_part, value_part, score_grad))
    return results


def backward_kernel(sizes, box_counts, *refs):
    n = len(SAVED)
    grads, encoder, languages, sources, ids_in, outer_grads = refs[:6]
    wholes = refs[6:16]
    self_weights, cross_weights = refs[16:18]
    saved = dict(zip(SAVED, refs[18 : 18 + n]))
    at = 18 + n
    hidden_out, hidden_grad, encoder_grad, small_out, packed_out = refs[at : at + 5]
    at += 5
    squares, outers, core_boxes = refs[at : at + 3]
    at += 3
    boxes = []
    for count in box_counts:
        boxes.append(refs[at : at + count])
        at += count
    small_box, pool, pairs_in, run_a, run_b, run_c, w, wo, stage, score_sum, bucket_rows, table, self_rows, cross_rows, ids, packed = refs[at : at + 16]
    send_sem, recv_sem, small_send, small_recv, load_sem, store_sem = refs[at + 16 :]
    place = Place(sizes)
    length = ids.shape[0]
    seqs, tokens = languages.shape[0], pool.shape[1]
    width = pool.shape[2]
    blocks = tokens // 128
    per_seq = width // PAIR
    sending = Pool(send_sem, send_sem.shape[0])
    loading = Pool(load_sem, load_sem.shape[0])
    storing = Pool(store_sem, store_sem.shape[0])

    def load(source, target):
        return PooledCopy(loading, source, target)

    def store(source, target):
        PooledCopy(storing, source, target)

    X = [pool.at[i] for i in range(11)] + [pairs_in.at[i] for i in range(4)]
    og, tn = X[0], X[1]
    get_og = load(grads, og)
    def outer_chunk(q):
        return wholes[9].at[q // 2, q % 2]

    def inner_chunk(q):
        return wholes[8].at[:, :, :, :, :, pl.ds(q * width, width)]

    arriving = {}

    def fetch(weights, pairs, key_rows, base):
        per_slot = stage.shape[1] // key_rows
        for n, p in enumerate(pairs):
            for s in range(seqs):
                at = base * per_slot + n * seqs + s
                part = stage.at[at // per_slot, pl.ds(at % per_slot * key_rows, key_rows)]
                arriving[key_rows, p, s] = load(weights.at[s * per_seq + p], part), part

    get_wo = [load(outer_chunk(0), wo.at[0])]
    get_slope = [load(saved["slope"].at[0], X[6])]
    get_tn = load(saved["third_norm"], tn)
    get_wi = [load(inner_chunk(0), w.at[0])]
    get_outers = load(outer_grads.at[:, place.c], outers)
    got = {}

    def load_more(q):
        if q < 3:
            get_slope.append(load(saved["slope"].at[q + 1], X[7 + q]))
        if q == 0:
            get_wo.append(load(outer_chunk(1), wo.at[1]))
            get_wi.append(load(inner_chunk(1), w.at[1]))
            got["table"] = load(saved["table"], table)
            got["late"] = load(saved["late"], run_c)
        if q == 1:
            got["cross_context"] = load(saved["cross_context"], X[2])
            got["co"] = load(wholes[7], w.at[2])
            got["cross_rows"] = load(saved["cross_rows"], cross_rows)
            got["cross_queries"] = load(saved["cross_queries"], X[3])
        if q == 2:
            got["keys"] = load(saved["source_keys"], pairs_in.at[pl.ds(0, 2)])
            got["values"] = load(saved["source_values"], pairs_in.at[pl.ds(2, 2)])
            fetch(cross_weights, (0,), stage.shape[1], 0)
        if q == 3:
            got["cq_w"] = load(wholes[4], w.at[3])
            got["second_norm"] = load(saved["second_norm"], X[4])
            got["first_norm"] = load(saved["first_norm"], X[5])
            got["self_rows"] = load(saved["self_rows"], self_rows)

    neighbour_barrier(place, far=True)

    def view_of(m):
        if m < 4:
            return lambda index: outers.at[(index[0],) + index[2:] + (m,)]
        return lambda index: squares.at[(m - 4,) + index]

    def leaving_of(m):
        if m < 4:
            return lambda core: outer_grads.at[:, core, :, :, m]
        return lambda core: squares.at[m - 4, :, core]

    exchange = Exchange(place, sending, recv_sem)
    plans = []
    for m in range(16):
        group, kind = m // 4, BACK_PATHS.index(BACKWARD_PATHS[m])
        slot = group % 2
        plans.append(
            Summed(
                place, BACK_PATHS[kind], view_of(m), leaving_of(m), core_boxes.at[slot, kind], [box.at[slot] for box in boxes[kind]],
                exchange,
            )
        )

    def put(i, value):
        squares[i] = value.reshape(squares.shape[1:]).astype(LOW)

    small_out[...] = jnp.zeros_like(small_out)

    def norm_backward(state, inflow, gain_row, before, after):
        def body(at):
            hidden, flow, gain = state[at, :], inflow[at, :], table[gain_row : gain_row + 1, :]
            scale = lax.rsqrt(jnp.mean(hidden * hidden, axis=-1, keepdims=True) + EPSILON)
            unit = hidden * scale
            small_out[gain_row : gain_row + 1, :] += jnp.sum(flow * unit, axis=0, keepdims=True)
            flow = flow * gain
            flow = (flow - unit * jnp.mean(unit * flow, axis=-1, keepdims=True)) * scale
            after[at, :] = before[at, :].astype(FULL) + flow

        each(blocks, body)

    branch = X[1]

    eg = X[10]

    def expanded_grad(q):
        if q == 0:
            get_og.wait()
        get_wo[q].wait()
        get_slope[q].wait()
        out_w = wo[q % 2].reshape(width, width)
        eg[...] = (nt_dot(og[...], out_w) * X[6 + q][...].astype(FULL)).astype(LOW)
        load_more(q)
        get_wo.append(load(outer_chunk((q + 2) % 4), wo.at[q % 2]))

    def inner_grad(q):
        get_tn.wait()
        put(q, tn_dot(tn[...], eg[...]))

    def third_grad(q):
        get_wi[q].wait()
        back = nt_dot(eg[...], flat(w.at[q % 2]))
        if q == 0:
            run_b[...] = back
        else:
            run_b[...] += back
        if q + 2 < 4:
            get_wi.append(load(inner_chunk(q + 2), w.at[q % 2]))
        if q == 3:
            got["so"] = load(wholes[3], w.at[0])
            got["q_w"] = load(wholes[0], w.at[1])
            got["encoder"] = load(encoder, pool.at[pl.ds(6, 2)])

    def third_backward():
        got["table"].wait()
        got["late"].wait()
        norm_backward(run_c, run_b, 10, og, run_a)
        got["inverse"] = load(saved["cross_inverse"], run_c)
        branch[...] = run_a[...].astype(LOW)

    def context_grad(weight, slot):
        got[weight].wait()
        got["inverse"].wait()
        X[0][...] = (nt_dot(branch[...], flat(w.at[slot])).astype(LOW).astype(FULL) * run_c[...]).astype(LOW)

    def cross_out_grad():
        got["cross_context"].wait()
        put(4, tn_dot(X[2][...], branch[...]))

    def cross_context_grad():
        context_grad("co", 2)
        got["k_w"] = load(wholes[1], w.at[2])
        got["mid"] = load(saved["mid"], run_c)

    def attention(rows, key_rows, pairs, one, finish_pair, ahead):
        for p in pairs:
            for s in range(seqs):
                arriving[key_rows, p, s][0].wait()
        ahead()
        items = []
        for p in pairs:
            for s in range(seqs):
                queries, keys, values, grad = one(s, pl.ds(p * PAIR, PAIR))
                items.append(
                    (arriving[key_rows, p, s][1][...], queries, keys, values, grad, rows[s * per_seq + p])
                )
        results = pairs_backward(items)
        for n, p in enumerate(pairs):
            finish_pair(p, pl.ds(p * PAIR, PAIR), results[n * seqs : (n + 1) * seqs])

    enc_length = pool.shape[1]

    def cross_attention(p):
        if p == 0:
            for name in ("cross_rows", "cross_queries", "keys", "values"):
                got[name].wait()

        def one(s, lanes):
            at = pl.ds(s * length, length)
            source = sources[s]
            return X[3][at, lanes], pairs_in[source, :, lanes], pairs_in[2 + source, :, lanes], X[0][at, lanes]

        def finish_pair(p, lanes, results):
            for s in range(seqs):
                X[1][pl.ds(s * length, length), lanes] = results[s][0].astype(LOW)
            for e in range(2):
                for target, part_at in ((8, 1), (11, 2)):
                    total = jnp.where(sources[0] == e, results[0][part_at], 0.0)
                    total = total + jnp.where(sources[1] == e, results[1][part_at], 0.0)
                    pool[target + e, :, lanes] = total.astype(LOW)

        def ahead():
            if p + 1 < per_seq:
                fetch(cross_weights, (p + 1,), enc_length, (p + 1) % 2 * 2)
            else:
                fetch(self_weights, (0, 1), length, 0)

        attention(cross_rows, enc_length, (p,), one, finish_pair, ahead)
        if p + 1 < per_seq:
            return
        got["queries"] = load(saved["queries"], X[11])
        got["keys"] = load(saved["keys"], X[12])
        got["values"] = load(saved["values"], X[13])
        got["self_context"] = load(saved["self_context"], X[14])

    def cross_query_grad():
        got["second_norm"].wait()
        put(5, tn_dot(X[4][...], X[1][...]))

    def source_grad(i, target):
        copy = got.pop("encoder", None)
        if copy is not None:
            copy.wait()
        put(i, tn_dot(pool[6], pool[target]) + tn_dot(pool[7], pool[target + 1]))

    def second_grad():
        got["cq_w"].wait()
        run_b[...] = nt_dot(X[1][...], flat(w.at[3]))
        got["v_w"] = load(wholes[2], w.at[3])

    def second_backward():
        got["mid"].wait()
        norm_backward(run_c, run_b, 9, run_a, run_a)
        got["inverse"] = load(saved["self_inverse"], run_c)
        branch[...] = run_a[...].astype(LOW)

    def self_out_grad():
        got["self_context"].wait()
        put(8, tn_dot(X[14][...], branch[...]))

    def self_context_grad():
        context_grad("so", 0)
        got["ck_w"] = load(wholes[5], w.at[0])
        got["start"] = load(saved["start"], run_c)

    def self_attention(turn):
        if turn == 0:
            for name in ("self_rows", "queries", "keys", "values"):
                got[name].wait()

        def one(s, lanes):
            at = pl.ds(s * length, length)
            return tuple(X[i][at, lanes] for i in (11, 12, 13, 0))

        def finish_pair(p, lanes, results):
            for s in range(seqs):
                for i in range(3):
                    X[2 + i][pl.ds(s * length, length), lanes] = results[s][i].astype(LOW)
            score_sum[p] = (results[0][3].astype(FULL) + results[1][3].astype(FULL)).astype(LOW)

        def ahead():
            if turn < 2:
                fetch(self_weights, (2 * turn + 2, 2 * turn + 3), length, (turn + 1) % 2 * 2)

        attention(self_rows, length, (2 * turn, 2 * turn + 1), one, finish_pair, ahead)

    def self_grad(i):
        copy = got.pop("first_norm", None)
        if copy is not None:
            copy.wait()
        put(9 + i, tn_dot(X[5][...], X[2 + i][...]))

    def closing_product(i):
        got[("q_w", "k_w", "v_w")[i]].wait()
        back = nt_dot(X[2 + i][...], flat(w.at[1 + i]))
        if i == 0:
            run_b[...] = back
            got["cv_w"] = load(wholes[6], w.at[1])
        else:
            run_b[...] += back

    def closing():
        got["start"].wait()
        got["activated"] = [load(saved["activated"].at[q], X[i]) for q, i in enumerate((0, 1, 5, 10))]
        norm_backward(run_c, run_b, 8, run_a, run_a)
        store(run_a, hidden_grad)
        got["late"] = load(saved["late"], run_c)
        for s in range(seqs):
            row = jnp.sum(run_a[pl.ds(s * length, length), :], axis=0, keepdims=True)
            for l in range(8):
                small_out[l : l + 1, :] += jnp.where(languages[s] == l, row, 0.0)

    def hidden_end(q):
        got["activated"][q].wait()
        get_wo[4 + q].wait()
        value = jnp.dot(X[(0, 1, 5, 10)[q]][...], wo[q % 2].reshape(width, width), preferred_element_type=FULL)
        if q < 2:
            get_wo.append(load(outer_chunk(q + 2), wo.at[q % 2]))
        if q == 0:
            got["late"].wait()
        if q < 3:
            run_c[...] += value
        else:
            X[2][...] = (run_c[...] + value).astype(LOW)
            store(X[2], hidden_out)

    def encoder_end(e, value):
        run = (run_b, run_c)[e]
        if value:
            got["cv_w"].wait()
            run[...] += nt_dot(pool[11 + e], flat(w.at[1]))
            store(run, encoder_grad.at[e])
        else:
            got["ck_w"].wait()
            run[...] = nt_dot(pool[8 + e], flat(w.at[0]))

    def bucket_sums(turn):
        if turn == 0:
            ids[...] = ids_in[...].astype(FULL).T.astype(jnp.int32)
        half = length // 2
        rows = 32

        def pair(p, _):
            def bucket_group(first, count, spans):
                sums = [[jnp.zeros((8, half), FULL) for _ in range(2)] for _ in range(count)]
                for n, side in spans:
                    block = pl.ds(n * rows, rows)
                    bucket = ids[block, side * half : (side + 1) * half]
                    scores = [
                        score_sum[p, block, h * length + side * half : h * length + (side + 1) * half].astype(FULL)
                        for h in range(2)
                    ]
                    for c in range(count):
                        here = bucket == first + c
                        for h in range(2):
                            kept = jnp.where(here, scores[h], 0.0).reshape(rows // 8, 8, half)
                            sums[c][h] = sums[c][h] + jnp.sum(kept, axis=0)
                for c in range(count):
                    for h in range(2):
                        row = (2 * p + h) * 32 + first + c
                        bucket_rows[pl.ds(row, 1), :] = jnp.sum(sums[c][h], axis=0, keepdims=True)

            blocks_of = length // rows
            every = [(n, side) for side in range(2) for n in range(blocks_of) if n * rows < (side + 1) * half]
            near = [(n, side) for n, side in every if n * rows + rows + 15 > side * half]
            for first in range(0, 32, 4):
                bucket_group(first, 4, near if first < 16 else every)
            return 0

        pair(turn, 0)
        if turn + 1 < per_seq:
            return
        ones = jnp.ones((8, 128), FULL)
        totals = lax.dot_general(
            ones, bucket_rows[...], (((1,), (1,)), ((), ())), precision=PRECISE, preferred_element_type=FULL
        )
        small_out[11:12, : bucket_rows.shape[0]] = totals[:1, :]

    small = []
    for dim in "cxyz":
        here, reach = place.at(dim), 1
        while reach < place.size(dim):
            small.append((dim, here + reach - 2 * reach * lax.rem(lax.div(here, reach), 2)))
            reach *= 2

    def small_copy(i):
        dim, partner = small[i]
        return pltpu.make_async_remote_copy(
            small_out, small_box.at[i], small_send.at[i], small_recv.at[i],
            device_id=place.device(dim, partner), device_id_type=MESH,
        )

    class Small:
        def start(self, i):
            small_copy(i).start()

        def finish(self, i):
            small_copy(i).wait()
            small_out[...] += small_box[i]

    tasks = dict(n3=third_backward, co=cross_out_grad, ccg=cross_context_grad, cq=cross_query_grad, n2a=second_grad, n2=second_backward)
    tasks.update(so=self_out_grad, scg=self_context_grad, cl1=closing)
    for e in range(2):
        tasks[f"e{e}k"] = functools.partial(encoder_end, e, False)
        tasks[f"e{e}v"] = functools.partial(encoder_end, e, True)
    tasks["ck"] = functools.partial(source_grad, 6, 8)
    tasks["cv"] = functools.partial(source_grad, 7, 11)
    for i in range(4):
        tasks[f"x{i}"] = functools.partial(expanded_grad, i)
        tasks[f"in{i}"] = functools.partial(inner_grad, i)
        tasks[f"t{i}"] = functools.partial(third_grad, i)
        tasks[f"h{i}"] = functools.partial(hidden_end, i)
    for i in range(per_seq):
        tasks[f"ca{i}"] = functools.partial(cross_attention, i)
        tasks[f"bk{i}"] = functools.partial(bucket_sums, i)
    for i in range(3):
        tasks[f"sa{i}"] = functools.partial(self_attention, i)
        tasks[f"cp{i}"] = functools.partial(closing_product, i)
        tasks["qkv"[i]] = functools.partial(self_grad, i)
    steps = [len(plan.stages) for plan in plans] + [len(small)]
    plans.append(Small())
    at = [0] * 17
    def keep_sum(m):
        plan = plans[m]
        packed[m] = plan.blocks(plan.own)[...].astype(FULL)
        store(packed.at[m], packed_out.at[m])

    for entry in BACKWARD_ORDER:
        if isinstance(entry, str):
            tasks[entry]()
            continue
        step = at[entry]
        at[entry] += 1
        if step >= 1:
            if entry < 4:
                get_outers.wait()
            plans[entry].finish(step - 1)
        if step < steps[entry]:
            plans[entry].start(step)
        elif entry < 16:
            keep_sum(entry)
    sending.drain()
    storing.drain()


def backward(sizes, output_grad, encoder_states, language_ids, source_index, bucket_ids, forward_outs):
    ny, nz = sizes
    grid = (ny, 2, nz, 2)
    tokens, width = output_grad.shape
    length = bucket_ids.shape[0]
    part = width // (ny * nz * 4)
    outer_grads, wholes, score_weights = forward_outs[0], forward_outs[1:11], forward_outs[11:13]
    saved = dict(zip(SAVED, forward_outs[13:]))
    enc_count, enc_length = encoder_states.shape[:2]
    anywhere = pl.BlockSpec(memory_space=pl.ANY)
    vmem = pl.BlockSpec(memory_space=pltpu.VMEM)
    smem = pl.BlockSpec(memory_space=pltpu.SMEM)
    lead = [sum_boxes(sizes, path)[0] for path in BACK_PATHS]
    receives = sum(sum_boxes(sizes, path)[1] for path in BACKWARD_PATHS)
    hops = (ny * nz * 4).bit_length() - 1
    pairs = tokens // length * (width // PAIR)
    row = (tokens, width)
    out_shape = [
        jax.ShapeDtypeStruct(row, LOW),
        jax.ShapeDtypeStruct(row, FULL),
        jax.ShapeDtypeStruct((enc_count, enc_length, width), FULL),
        jax.ShapeDtypeStruct((16, width), FULL),
        jax.ShapeDtypeStruct((16, part, width), FULL),
    ]
    outs = pl.pallas_call(
        functools.partial(backward_kernel, sizes, tuple(len(s) for s in lead)),
        out_shape=out_shape,
        in_specs=[anywhere, anywhere, smem, smem, vmem] + [anywhere] * (13 + len(SAVED)),
        out_specs=[anywhere] * 3 + [vmem, anywhere],
        scratch_shapes=[
            pltpu.VMEM((12,) + grid + (part, width), LOW),
            pltpu.VMEM((ny, nz, 2, 4, part, width), LOW),
            pltpu.VMEM((2, 4, ny, nz, 2, part, width), LOW),
        ]
        + [pltpu.VMEM((2,) + s + (part, width), LOW) for one in lead for s in one]
        + [
            pltpu.VMEM((hops, 16, width), FULL),
            pltpu.VMEM((13,) + row, LOW),
            pltpu.VMEM((4,) + row, LOW),
            pltpu.VMEM(row, FULL),
            pltpu.VMEM(row, FULL),
            pltpu.VMEM(row, FULL),
            pltpu.VMEM((4,) + grid + (part, width), LOW),
            pltpu.VMEM((2, nz, 2, 4, part, width), LOW),
            pltpu.VMEM((4, enc_length, 2 * length), LOW),
            pltpu.VMEM((width // PAIR, length, 2 * length), LOW),
            pltpu.VMEM((32 * H, 128), FULL),
            pltpu.VMEM((16, width), FULL),
            pltpu.VMEM((pairs, 1, 2 * length), FULL),
            pltpu.VMEM((pairs, 1, 2 * length), FULL),
            pltpu.VMEM((length, length), jnp.int32),
            pltpu.VMEM((16, part, width), FULL),
            pltpu.SemaphoreType.DMA((40,)),
            pltpu.SemaphoreType.DMA((receives,)),
            pltpu.SemaphoreType.DMA((hops,)),
            pltpu.SemaphoreType.DMA((hops,)),
            pltpu.SemaphoreType.DMA((28,)),
            pltpu.SemaphoreType.DMA((8,)),
        ],
        compiler_params=pltpu.CompilerParams(
            collective_id=3, has_side_effects=True, vmem_limit_bytes=63 * 1024 * 1024
        ),
    )(
        output_grad, encoder_states, language_ids, source_index, bucket_ids, outer_grads, *wholes, *score_weights,
        *[saved[name] for name in SAVED],
    )
    return finish(sizes, outs)


def finish_kernel(sizes, *refs):
    hidden_out, hidden_grad, encoder_grad, small_in, packed_in = refs[:5]
    outs = refs[5:18]
    language, bucket, gains = refs[18], refs[19], refs[20:23]
    staged_hidden, staged_grad, staged_encoder, small, packed, sem, in_sem = refs[23:]
    part, width = packed.shape[1:]
    copies, arriving = [], []

    def copy(source, target):
        copies.append(pltpu.make_async_copy(source, target, sem.at[len(copies)]))
        copies[-1].start()

    def arrive(source, target):
        arriving.append(pltpu.make_async_copy(source, target, in_sem.at[len(arriving)]))
        arriving[-1].start()
        return arriving[-1]

    get_small = arrive(small_in, small)
    blocks = []
    for source, target, out, pieces in (
        (encoder_grad, staged_encoder, outs[2], 4), (hidden_grad, staged_grad, outs[1], 2),
        (hidden_out, staged_hidden, outs[0], 1),
    ):
        size = source.shape[-2]
        for n in range(pieces):
            if len(source.shape) == 3:
                half = size // 2
                index = (n // 2, pl.ds(n % 2 * half, half))
            else:
                index = pl.ds(n * (size // pieces), size // pieces)
            blocks.append((arrive(source.at[index], target.at[index]), target.at[index], out.at[index]))
    groups = [arrive(packed_in.at[pl.ds(4 * n, 4)], packed.at[pl.ds(4 * n, 4)]) for n in range(4)]
    for ready, source, target in blocks:
        ready.wait()
        copy(source, target)
    for group in groups:
        group.wait()
    for q in range(4):
        copy(packed.at[q], outs[12].at[pl.ds(q * part, part)])
        copy(packed.at[4 + q], outs[11].at[:, pl.ds(q * width, width)])
    for i, m in enumerate((13, 14, 15, 12, 9, 10, 11, 8)):
        copy(packed.at[m], outs[3 + i])
    get_small.wait()
    place = Place(sizes)
    start = (place.dp * sizes[1] * 2 + place.fs) * part
    row = lax.broadcasted_iota(jnp.int32, (width, 128), 0)
    lane = lax.broadcasted_iota(jnp.int32, (width, 128), 1)
    chosen = jnp.where((row == lane + start) & (lane < part), 1.0, 0.0)
    own = jnp.dot(small[...], chosen, precision=PRECISE, preferred_element_type=FULL)
    language[...] = own[:8, :part]
    for i in range(3):
        gains[i][...] = own[8 + i, :part]
    row = lax.broadcasted_iota(jnp.int32, (16, width), 0)
    lane = lax.broadcasted_iota(jnp.int32, (16, width), 1)
    spread = jnp.where(lax.div(lane, 32) == row, small[11:12, :], 0.0)
    row = lax.broadcasted_iota(jnp.int32, (width, 128), 0)
    lane = lax.broadcasted_iota(jnp.int32, (width, 128), 1)
    places = jnp.where(lax.rem(row, 32) == lane, 1.0, 0.0)
    bucket[...] = jnp.dot(spread, places, precision=PRECISE, preferred_element_type=FULL)[:H, :32]
    for c in copies:
        c.wait()


def finish(sizes, outs):
    part, width = outs[4].shape[1:]
    anywhere = pl.BlockSpec(memory_space=pl.ANY)
    hbm = pl.BlockSpec(memory_space=pltpu.HBM)
    vmem = pl.BlockSpec(memory_space=pltpu.VMEM)
    shapes = [o.shape for o in outs[:3]] + [(part, width)] * 8
    shapes += [(part, 4 * width), (4 * part, width)]
    out_shape = [jax.ShapeDtypeStruct(s, FULL) for s in shapes]
    out_shape[0] = jax.ShapeDtypeStruct(shapes[0], LOW)
    out_shape += [jax.ShapeDtypeStruct(s, FULL) for s in ((8, part), (H, 32), (part,), (part,), (part,))]
    return pl.pallas_call(
        functools.partial(finish_kernel, sizes),
        out_shape=out_shape,
        in_specs=[hbm] * 5,
        out_specs=[anywhere] * 13 + [vmem] * 5,
        scratch_shapes=[pltpu.VMEM(o.shape, o.dtype) for o in outs]
        + [pltpu.SemaphoreType.DMA((23,)), pltpu.SemaphoreType.DMA((12,))],
        compiler_params=pltpu.CompilerParams(vmem_limit_bytes=60 * 1024 * 1024),
    )(*outs)


def local_general(
    sizes,
    hidden_in,
    output_grad,
    encoder_states,
    language_ids,
    source_index,
    bucket_ids,
    language_table,
    bucket_table,
    self_gain,
    self_query,
    self_key,
    self_value,
    self_out,
    cross_gain,
    cross_query,
    cross_key,
    cross_value,
    cross_out,
    feed_gain,
    inner_weight,
    outer_weight,
):
    seq_count = language_ids.shape[0]
    length = bucket_ids.shape[0]
    tokens = seq_count * length
    enc_count = encoder_states.shape[0]
    enc_length = encoder_states.shape[1]
    width = hidden_in.shape[1]
    blocks = seq_count // SEQ_BLOCK
    (
        gain_one, gain_two, gain_three, table_whole, query_whole, key_whole, value_whole, out_whole,
        cquery_whole, ckey_whole, cvalue_whole, cout_whole, inner_whole, outer_whole,
    ) = gather_weights(
        sizes, language_table, (self_gain, cross_gain, feed_gain),
        (self_query, self_key, self_value, self_out, cross_query, cross_key, cross_value, cross_out),
        inner_weight, outer_weight,
    )

    def to_blocks(array, rows):
        return array.reshape(blocks, SEQ_BLOCK, rows, array.shape[-1])

    language_hot = (language_ids[:, None] == jnp.arange(table_whole.shape[0])[None, :]).astype(
        jnp.float32
    )
    language_rows = jnp.dot(language_hot, table_whole.astype(jnp.float32), precision=PRECISE)
    start_state = (
        hidden_in.astype(jnp.float32).reshape(seq_count, length, width) + language_rows[:, None, :]
    ).reshape(tokens, width)
    first_norm = to_low(norm_scale(start_state, gain_one.astype(jnp.float32)))
    self_queries = to_low(matmul(first_norm, query_whole))
    self_keys = to_low(matmul(first_norm, key_whole))
    self_values = to_low(matmul(first_norm, value_whole))
    bucket_hot = (
        bucket_ids[:, :, None] == jnp.arange(bucket_table.shape[0])[None, None, :]
    ).astype(jnp.float32)
    position_bias = jnp.einsum(
        "ijb,bh->hij", bucket_hot, bucket_table.astype(jnp.float32), precision=PRECISE
    )
    positions = jnp.arange(length)
    masked_bias = jnp.where(
        (positions[:, None] >= positions[None, :])[None], position_bias, NEGATIVE
    )

    def self_forward(block_items):
        return attend_forward(block_items[0], block_items[1], block_items[2], masked_bias)

    self_context, self_total = lax.map(
        self_forward,
        (
            to_blocks(self_queries, length),
            to_blocks(self_keys, length),
            to_blocks(self_values, length),
        ),
    )
    self_context = self_context.reshape(tokens, -1)
    mid_state = start_state + matmul(self_context, out_whole)
    second_norm = to_low(norm_scale(mid_state, gain_two.astype(jnp.float32)))
    cross_queries = to_low(matmul(second_norm, cquery_whole))
    encoder_flat = encoder_states.reshape(enc_count * enc_length, width)
    source_keys = to_low(matmul(encoder_flat, ckey_whole)).reshape(enc_count, enc_length, -1)
    source_values = to_low(matmul(encoder_flat, cvalue_whole)).reshape(enc_count, enc_length, -1)
    source_hot = (source_index[:, None] == jnp.arange(enc_count)[None, :]).astype(jnp.float32)
    source_low = to_low(source_hot)
    picked_keys = to_low(
        jnp.einsum("se,emc->smc", source_low, source_keys, preferred_element_type=jnp.float32)
    )
    picked_values = to_low(
        jnp.einsum("se,emc->smc", source_low, source_values, preferred_element_type=jnp.float32)
    )

    def cross_forward(block_items):
        return attend_forward(block_items[0], block_items[1], block_items[2], 0.0)

    cross_context, cross_total = lax.map(
        cross_forward,
        (
            to_blocks(cross_queries, length),
            picked_keys.reshape(blocks, SEQ_BLOCK, enc_length, -1),
            picked_values.reshape(blocks, SEQ_BLOCK, enc_length, -1),
        ),
    )
    cross_context = cross_context.reshape(tokens, -1)
    late_state = mid_state + matmul(cross_context, cout_whole)
    third_norm = to_low(norm_scale(late_state, gain_three.astype(jnp.float32)))
    expanded = matmul(third_norm, inner_whole)
    activated = to_low(jax.nn.gelu(expanded, approximate=True))
    hidden_out = (late_state + matmul(activated, outer_whole)).astype(jnp.bfloat16)
    top_grad = output_grad.astype(jnp.float32)
    outer_full = left_product(activated, output_grad)
    activated_grad = right_product(output_grad, outer_whole)
    gelu_value, gelu_back = jax.vjp(jax.nn.gelu, expanded)
    expanded_grad = to_low(gelu_back(activated_grad)[0])
    inner_full = left_product(third_norm, expanded_grad)
    third_grad = right_product(expanded_grad, inner_whole)
    norm_value, norm_back = jax.vjp(norm_scale, late_state, gain_three.astype(jnp.float32))
    state_back, feed_gain_full = norm_back(third_grad)
    late_grad = top_grad + state_back
    cross_low = to_low(late_grad)
    cout_full = left_product(cross_context, cross_low)
    cross_context_grad = to_low(right_product(cross_low, cout_whole))

    def cross_backward(block_items):
        return attend_backward(
            block_items[0],
            block_items[1],
            block_items[2],
            0.0,
            block_items[3],
            block_items[4],
            False,
        )

    cquery_part, ckey_part, cvalue_part = lax.map(
        cross_backward,
        (
            to_blocks(cross_queries, length),
            picked_keys.reshape(blocks, SEQ_BLOCK, enc_length, -1),
            picked_values.reshape(blocks, SEQ_BLOCK, enc_length, -1),
            cross_total,
            to_blocks(cross_context_grad, length),
        ),
    )
    cquery_low = to_low(cquery_part.reshape(tokens, -1))
    source_key_grad = to_low(
        jnp.einsum(
            "se,smc->emc",
            source_hot,
            ckey_part.reshape(seq_count, enc_length, -1),
            precision=PRECISE,
        ).reshape(enc_count * enc_length, -1)
    )
    source_value_grad = to_low(
        jnp.einsum(
            "se,smc->emc",
            source_hot,
            cvalue_part.reshape(seq_count, enc_length, -1),
            precision=PRECISE,
        ).reshape(enc_count * enc_length, -1)
    )
    cquery_full = left_product(second_norm, cquery_low)
    ckey_full = left_product(encoder_flat, source_key_grad)
    cvalue_full = left_product(encoder_flat, source_value_grad)
    encoder_grad = (
        right_product(source_key_grad, ckey_whole) + right_product(source_value_grad, cvalue_whole)
    ).reshape(enc_count, enc_length, width)
    second_grad = right_product(cquery_low, cquery_whole)
    norm_value, norm_back = jax.vjp(norm_scale, mid_state, gain_two.astype(jnp.float32))
    state_back, cross_gain_full = norm_back(second_grad)
    mid_grad = late_grad + state_back
    self_low = to_low(mid_grad)
    out_full = left_product(self_context, self_low)
    self_context_grad = to_low(right_product(self_low, out_whole))

    def self_backward(block_items):
        return attend_backward(
            block_items[0],
            block_items[1],
            block_items[2],
            masked_bias,
            block_items[3],
            block_items[4],
            True,
        )

    query_part, key_part, value_part, bias_part = lax.map(
        self_backward,
        (
            to_blocks(self_queries, length),
            to_blocks(self_keys, length),
            to_blocks(self_values, length),
            self_total,
            to_blocks(self_context_grad, length),
        ),
    )
    query_low = to_low(query_part.reshape(tokens, -1))
    key_low = to_low(key_part.reshape(tokens, -1))
    value_low = to_low(value_part.reshape(tokens, -1))
    table_full = jnp.einsum(
        "hij,ijb->bh", jnp.sum(bias_part, axis=0), bucket_hot, precision=PRECISE
    )
    query_full = left_product(first_norm, query_low)
    key_full = left_product(first_norm, key_low)
    value_full = left_product(first_norm, value_low)
    first_grad = (
        right_product(query_low, query_whole)
        + right_product(key_low, key_whole)
        + right_product(value_low, value_whole)
    )
    norm_value, norm_back = jax.vjp(norm_scale, start_state, gain_one.astype(jnp.float32))
    state_back, self_gain_full = norm_back(first_grad)
    hidden_in_grad = mid_grad + state_back
    sequence_sums = jnp.sum(hidden_in_grad.reshape(seq_count, length, width), axis=1)
    language_full = left_product(language_hot, sequence_sums)
    (
        language_part, bucket_table_grad, sgain_part, cgain_part, feed_gain_part, whole_parts, inner_part, outer_part,
    ) = reduce_grads(
        sizes, language_full, table_full, (self_gain_full, cross_gain_full, feed_gain_full),
        (query_full, key_full, value_full, out_full, cquery_full, ckey_full, cvalue_full, cout_full),
        inner_full, outer_full,
    )
    query_sum, key_sum, value_sum, out_part, cquery_part_sum, ckey_part_sum, cvalue_part_sum, cout_part = whole_parts
    return (
        hidden_out,
        hidden_in_grad,
        encoder_grad,
        language_part,
        bucket_table_grad,
        sgain_part,
        query_sum,
        key_sum,
        value_sum,
        out_part,
        cgain_part,
        cquery_part_sum,
        ckey_part_sum,
        cvalue_part_sum,
        cout_part,
        feed_gain_part,
        inner_part,
        outer_part,
    )


def local(sizes, *args):
    if sizes == (2, 4) and args[8].shape[0] % 8 == 0:
        return local_fused(sizes, *args)
    return local_general(sizes, *args)


def local_fused(
    sizes, hidden_in, output_grad, encoder_states, language_ids, source_index, bucket_ids, language_table,
    bucket_table, self_gain, self_query, self_key, self_value, self_out, cross_gain, cross_query, cross_key,
    cross_value, cross_out, feed_gain, inner_weight, outer_weight,
):
    kept = forward(
        sizes, hidden_in, output_grad, encoder_states, language_ids, source_index, bucket_ids, language_table,
        bucket_table, (self_gain, cross_gain, feed_gain),
        (self_query, self_key, self_value, self_out, cross_query, cross_key, cross_value, cross_out),
        inner_weight, outer_weight,
    )
    outs = backward(sizes, output_grad, encoder_states, language_ids, source_index, bucket_ids, kept)
    squares, inner, outer, language, bucket, gains = outs[3:11], outs[11], outs[12], outs[13], outs[14].T, outs[15:]
    return (
        *outs[:3], language, bucket, gains[0], *squares[:4], gains[1], *squares[4:], gains[2], inner, outer,
    )


def solution(mesh):
    sizes = (mesh.shape["dp"] // 2, mesh.shape["fsdp"] // 2)
    in_specs = (
        P(("dp", "fsdp"), None),
        P(("dp", "fsdp"), None),
        P(("dp", "fsdp"), None, None),
        P(("dp", "fsdp")),
        P(("dp", "fsdp")),
        P(),
        P(None, ("dp", "fsdp")),
        P(),
        P(("dp", "fsdp")),
        P(("dp", "fsdp"), None),
        P(("dp", "fsdp"), None),
        P(("dp", "fsdp"), None),
        P(("dp", "fsdp"), None),
        P(("dp", "fsdp")),
        P(("dp", "fsdp"), None),
        P(("dp", "fsdp"), None),
        P(("dp", "fsdp"), None),
        P(("dp", "fsdp"), None),
        P(("dp", "fsdp")),
        P(("dp", "fsdp"), None),
        P(("dp", "fsdp"), None),
    )
    out_specs = (
        P(("dp", "fsdp"), None),
        P(("dp", "fsdp"), None),
        P(("dp", "fsdp"), None, None),
        P(None, ("dp", "fsdp")),
        P(),
        P(("dp", "fsdp")),
        P(("dp", "fsdp"), None),
        P(("dp", "fsdp"), None),
        P(("dp", "fsdp"), None),
        P(("dp", "fsdp"), None),
        P(("dp", "fsdp")),
        P(("dp", "fsdp"), None),
        P(("dp", "fsdp"), None),
        P(("dp", "fsdp"), None),
        P(("dp", "fsdp"), None),
        P(("dp", "fsdp")),
        P(("dp", "fsdp"), None),
        P(("dp", "fsdp"), None),
    )
    return jax.shard_map(functools.partial(local, sizes), mesh=mesh, in_specs=in_specs, out_specs=out_specs, check_vma=False)
```

profile of v0, /device:TPU:0, one launch (start us, length us, event | category | flops | bytes accessed | tf_op | source)
XLA Modules:
  0.0 179.2 jit_solution(15266733485928491257)
XLA Ops:
  0.7 1.4 convert_add_fusion.refs_0_.refs_17_
  2.0 83.4 %shard_map.340 = (bf16[2,2,4,2,4,24,768]{6,5,4,3,2,1,0:T(8,128)(2,1)}, bf16[2,2,4,2,24,768]{5,4,3,2,1,0:T(8,128)(2,1)}, bf16[2,2,4,2,24,768]{5,4,3,2,1,0:T(8,128...) custom-call(f32[32,128]{1,0:T(8,128)} %convert_add_fusion.refs_0_.re, ...), custom_call_target="tpu_custom_call" | custom-call | tf_op jit(solution)/shard_map/pallas_call | solution.py:1130
  85.4 86.9 %shard_map.341 = (bf16[512,768]{1,0:T(8,128)(2,1)}, f32[512,768]{1,0:T(8,128)}, f32[2,512,768]{2,1,0:T(8,128)}, f32[16,768]{1,0:T(8,128)}, f32[16,24,768]{2,1,0:T(8,128)}) custom-call(bf16[512,768]{1,0:T(8,128)(2,1)} %refs_0_.1, bf16[2,512,768]{2,1,0:T(8,128)(2,1)} %refs_1_.3, s32[2]{0:T(128)} %refs_2_.3, s32[2]{0:T(128)} %refs_3_.3, s32[256,256]{1,0:T(8,128)} %refs_4_.3, ...), custom_call_target="tpu_custom_call" | custom-call | tf_op jit(solution)/shard_map/pallas_call | solution.py:1741
  172.3 6.5 %shard_map.342 = (bf16[512,768]{1,0:T(8,128)(2,1)}, f32[512,768]{1,0:T(8,128)}, f32[2,512,768]{2,1,0:T(8,128)}, f32[24,768]{1,0:T(8,128)}, f32[24,768]{1,0:T(8,1...) custom-call(bf16[512,768]{1,0:T(8,128)(2,1)} %get-tuple-element.109., ...), custom_call_target="tpu_custom_call" | custom-call | tf_op jit(solution)/shard_map/pallas_call | solution.py:1859
where the time goes:
time: 182 us; the launch traced here: 179 us
  Pallas kernels  177 us (97%)
    pallas_call x1, Pallas kernels, backward(): pl.pallas_call(functools.partial(backward_kernel, sizes, tuple((len(s) fo...  86.9 us
    pallas_call x1, Pallas kernels, forward(): pl.pallas_call(functools.partial(forward_kernel, sizes), out_shape=out_sh...  83.4 us
    pallas_call x1, Pallas kernels, finish(): pl.pallas_call(functools.partial(finish_kernel, sizes), out_shape=out_sha...  6.49 us

commit v1 on v0

--- a/solution.py
+++ b/solution.py
@@ -923,6 +923,7 @@
         PooledCopy(moving, source, target)
         for source, target in ((hidden_in, hidden), (encoder_in, encoder), (upstream_in, upstream))
     ]
+    get_ids = PooledCopy(moving, ids, ids_across)
     neighbour_barrier(place)
     plans = gather_plans(place, wholes, tiny, Exchange(place, sending, recv_sem))
     for copy in owns:
@@ -1061,7 +1062,8 @@
 
     def bias_values(turn):
         if turn == 0:
-            ids_across[...] = ids[...].astype(FULL).T.astype(jnp.int32)
+            get_ids.wait()
+            ids_across[...] = ids_across[...].astype(FULL).T.astype(jnp.int32)
         build_bias(ids_across, slab_values, bias, (3 * turn, 3 * turn + 3))
 
     def outer_grad(q):
@@ -1130,7 +1132,7 @@
     outs = pl.pallas_call(
         functools.partial(forward_kernel, sizes),
         out_shape=out_shape,
-        in_specs=[anywhere] * 11 + [anywhere] * 3 + [smem, smem, vmem, smem],
+        in_specs=[anywhere] * 11 + [anywhere] * 3 + [smem, smem, anywhere, smem],
         out_specs=[anywhere] * len(out_shape),
         scratch_shapes=[pltpu.VMEM(w.shape, w.dtype) for w in wholes]
         + [pltpu.VMEM(*shapes[name]) for name in SAVED]
@@ -1142,7 +1144,7 @@
             pltpu.VMEM((tokens, width), LOW),
             pltpu.VMEM(encoder.shape, LOW),
             pltpu.VMEM((length, length), jnp.int32),
-            pltpu.SemaphoreType.DMA((48,)),
+            pltpu.SemaphoreType.DMA((36,)),
             pltpu.SemaphoreType.DMA((sum(RECEIVES[path] for path in FORWARD_PATHS),)),
             pltpu.SemaphoreType.DMA((28,)),
         ],
@@ -1358,6 +1360,7 @@
             got["second_norm"] = load(saved["second_norm"], X[4])
             got["first_norm"] = load(saved["first_norm"], X[5])
             got["self_rows"] = load(saved["self_rows"], self_rows)
+            got["ids"] = load(ids_in, ids)
 
     neighbour_barrier(place, far=True)
 
@@ -1607,7 +1610,8 @@
 
     def bucket_sums(turn):
         if turn == 0:
-            ids[...] = ids_in[...].astype(FULL).T.astype(jnp.int32)
+            got["ids"].wait()
+            ids[...] = ids[...].astype(FULL).T.astype(jnp.int32)
         half = length // 2
         rows = 32
 
@@ -1741,7 +1745,7 @@
     outs = pl.pallas_call(
         functools.partial(backward_kernel, sizes, tuple(len(s) for s in lead)),
         out_shape=out_shape,
-        in_specs=[anywhere, anywhere, smem, smem, vmem] + [anywhere] * (13 + len(SAVED)),
+        in_specs=[anywhere, anywhere, smem, smem, anywhere] + [anywhere] * (13 + len(SAVED)),
         out_specs=[anywhere] * 3 + [vmem, anywhere],
         scratch_shapes=[
             pltpu.VMEM((12,) + grid + (part, width), LOW),
@@ -1766,11 +1770,11 @@
             pltpu.VMEM((pairs, 1, 2 * length), FULL),
             pltpu.VMEM((length, length), jnp.int32),
             pltpu.VMEM((16, part, width), FULL),
-            pltpu.SemaphoreType.DMA((40,)),
+            pltpu.SemaphoreType.DMA((30,)),
             pltpu.SemaphoreType.DMA((receives,)),
             pltpu.SemaphoreType.DMA((hops,)),
             pltpu.SemaphoreType.DMA((hops,)),
-            pltpu.SemaphoreType.DMA((28,)),
+            pltpu.SemaphoreType.DMA((24,)),
             pltpu.SemaphoreType.DMA((8,)),
         ],
         compiler_params=pltpu.CompilerParams(

time: 182 us -> 181 us (level)
  no operation moved by 1% of the time
where the time goes in v1:
time: 181 us; the launch traced here: 179 us
  Pallas kernels  176 us (97%)
    pallas_call x1, Pallas kernels, backward(): pl.pallas_call(functools.partial(backward_kernel, sizes, tuple((len(s) fo...  86.4 us
    pallas_call x1, Pallas kernels, forward(): pl.pallas_call(functools.partial(forward_kernel, sizes), out_shape=out_sh...  83.1 us
    pallas_call x1, Pallas kernels, finish(): pl.pallas_call(functools.partial(finish_kernel, sizes), out_shape=out_sha...  6.49 us

profile of v1, /device:TPU:0, one launch (start us, length us, event | category | flops | bytes accessed | tf_op | source)
XLA Modules:
  0.0 178.6 jit_solution(1995374222806164839)
XLA Ops:
  0.7 1.4 convert_add_fusion.refs_0_.refs_17_
  2.0 83.1 %shard_map.340 = (bf16[2,2,4,2,4,24,768]{6,5,4,3,2,1,0:T(8,128)(2,1)}, bf16[2,2,4,2,24,768]{5,4,3,2,1,0:T(8,128)(2,1)}, bf16[2,2,4,2,24,768]{5,4,3,2,1,0:T(8,128...) custom-call(f32[32,128]{1,0:T(8,128)} %convert_add_fusion.refs_0_.re, ...), custom_call_target="tpu_custom_call" | custom-call | tf_op jit(solution)/shard_map/pallas_call | solution.py:1132
  85.2 86.4 %shard_map.341 = (bf16[512,768]{1,0:T(8,128)(2,1)}, f32[512,768]{1,0:T(8,128)}, f32[2,512,768]{2,1,0:T(8,128)}, f32[16,768]{1,0:T(8,128)}, f32[16,24,768]{2,1,0:T(8,128)}) custom-call(bf16[512,768]{1,0:T(8,128)(2,1)} %refs_0_.1, bf16[2,512,768]{2,1,0:T(8,128)(2,1)} %refs_1_.3, s32[2]{0:T(128)} %refs_2_.3, s32[2]{0:T(128)} %refs_3_.3, s32[256,256]{1,0:T(8,128)} %refs_4_.3, ...), custom_call_target="tpu_custom_call" | custom-call | tf_op jit(solution)/shard_map/pallas_call | solution.py:1745
  171.6 6.5 %shard_map.342 = (bf16[512,768]{1,0:T(8,128)(2,1)}, f32[512,768]{1,0:T(8,128)}, f32[2,512,768]{2,1,0:T(8,128)}, f32[24,768]{1,0:T(8,128)}, f32[24,768]{1,0:T(8,1...) custom-call(bf16[512,768]{1,0:T(8,128)(2,1)} %get-tuple-element.109., ...), custom_call_target="tpu_custom_call" | custom-call | tf_op jit(solution)/shard_map/pallas_call | solution.py:1863
